TPU v7x, 32 devices: a whole 2x2x4 slice. The times are simulated.
32 devices in a mesh: dp: 2 (over core), row: 4 (over z), col: 4 (over y, x).
Axes of the slice: x: 2, y: 2, z: 4, core: 2. Of those that a mesh axis runs over, the one named last changes fastest.
Arguments:
- tokens: bfloat16 [2048, 4096], P(('dp', 'col'), 'row'), may hold values from -6 to 6
- w_in: bfloat16 [4096, 16384], P('row', 'col'), may hold values from -0.09375 to 0.09375
- w_out: bfloat16 [16384, 4096], P('col', 'row'), may hold values from -0.046875 to 0.046875
- out_grad: bfloat16 [2048, 4096], P(('dp', 'col'), 'row'), may hold values from -6 to 6
Outputs:
- output: bfloat16 [2048, 4096], P(('dp', 'col'), 'row')
- grad_x: bfloat16 [2048, 4096], P(('dp', 'col'), 'row')
- grad_w_in: bfloat16 [4096, 4, 4096], P('row', 'col', 'dp')
- grad_w_out: bfloat16 [4, 4096, 4096], P('col', 'dp', 'row')
All inputs are finite; a program needn't handle non-finite values.
Results may differ from a plain program's by a relative error of at most 0.005.
Values may be sent and summed in bfloat16 or wider, within the bound.
No kernel may reach another device: no remote copies, remote signals or barrier semaphores. Data moves between devices by JAX's collectives and lax.ppermute only.
A program may use at most 128 MiB of HBM per device.

v0:
```python
import math

import jax
import jax.numpy as jnp
from jax import lax
from jax.sharding import PartitionSpec as P


def gelu_parts(pre):
    cdf = 0.5 * (1.0 + jax.scipy.special.erf(pre / math.sqrt(2.0)))
    pdf = jnp.exp(-0.5 * pre * pre) / math.sqrt(2.0 * math.pi)
    return (pre * cdf, cdf + pre * pdf)


def rows_times(left, right, transpose_right):
    if transpose_right:
        return lax.dot_general(
            left, right, (((1,), (1,)), ((), ())), preferred_element_type=jnp.float32
        )
    return jnp.dot(left, right, preferred_element_type=jnp.float32)


def on_device(tokens, w_in, w_out, out_grad):
    x_full, grad_full = (
        lax.all_gather(tokens, "col", axis=0, tiled=True),
        lax.all_gather(out_grad, "col", axis=0, tiled=True),
    )
    pre = lax.psum_scatter(rows_times(x_full, w_in, False), "row", scatter_dimension=0, tiled=True)
    act_value, slope = gelu_parts(pre)
    act_full = lax.all_gather(act_value.astype(jnp.bfloat16), "row", axis=0, tiled=True)
    grad_act = lax.psum_scatter(
        rows_times(grad_full, w_out, True), "row", scatter_dimension=0, tiled=True
    )
    pre_grad = (grad_act * slope).astype(jnp.bfloat16)
    pre_grad_full = lax.all_gather(pre_grad, "row", axis=0, tiled=True)
    in_term = lax.dot_general(
        x_full, pre_grad_full, (((0,), (0,)), ((), ())), preferred_element_type=jnp.float32
    )
    out_term = lax.dot_general(
        act_full, grad_full, (((0,), (0,)), ((), ())), preferred_element_type=jnp.float32
    )
    in_term = in_term.reshape(in_term.shape[0], 1, in_term.shape[1])
    out_term = out_term.reshape(1, out_term.shape[0], out_term.shape[1])
    output = lax.psum_scatter(
        rows_times(act_full, w_out, False), "col", scatter_dimension=0, tiled=True
    ).astype(jnp.bfloat16)
    grad_x = lax.psum_scatter(
        rows_times(pre_grad_full, w_in, True), "col", scatter_dimension=0, tiled=True
    ).astype(jnp.bfloat16)
    summed_in, summed_out = (
        lax.psum_scatter(in_term, "dp", scatter_dimension=2, tiled=True),
        lax.psum_scatter(out_term, "dp", scatter_dimension=1, tiled=True),
    )
    return (output, grad_x, summed_in.astype(jnp.bfloat16), summed_out.astype(jnp.bfloat16))


def solution(mesh):
    placed = (P(("dp", "col"), "row"), P("row", "col"), P("col", "row"), P(("dp", "col"), "row"))
    return jax.shard_map(
        on_device,
        mesh=mesh,
        in_specs=placed,
        out_specs=(
            P(("dp", "col"), "row"),
            P(("dp", "col"), "row"),
            P("row", "col", "dp"),
            P("col", "dp", "row"),
        ),
        check_vma=False,
    )
```

profile of v0, /device:TPU:0, one launch (start us, length us, event | category | flops | bytes accessed | tf_op | source)
XLA Modules:
  0.0 1139.7 jit_solution(9004341970975315115)
XLA Ops:
  8.7 39.2 %all-gather.9.cloned.1.call-done = bf16[1024,1024]{1,0:T(8,128)(2,1)} async-done(((bf16[256,1024]{1,0:T(8,128)(2,1)}), bf16[1024,1024]{1,0:T(8,128)(2,1)}) %all-gather.9.cloned.1.call-update) | async-done | bytes 2097168 | tf_op jit(solution)/shard_map/all_gather | solution.py:26
  47.9 16.0 %fusion.8 = f32[1024,4096]{1,0:T(8,128)} fusion(bf16[1024,1024]{1,0:T(8,128)(2,1)} %all-gather.9.cloned.1.call-done, bf16[4096,1024]{1,0:T(8,128)(2,1)} %param.6), kind=kOutput, calls=%fused_computation.13 | convolution fusion | flops 8589934592 | bytes 27262976 | tf_op jit(solution)/shard_map/dot_general | solution.py:17
  64.0 21.1 %all-gather.5.cloned.1.call-done = bf16[1024,1024]{1,0:T(8,128)(2,1)} async-done(((bf16[256,1024]{1,0:T(8,128)(2,1)}), bf16[1024,1024]{1,0:T(8,128)(2,1)}) %all-gather.5.cloned.1.call-update) | async-done | bytes 2097168 | tf_op jit(solution)/shard_map/all_gather | solution.py:25
  85.1 16.0 %fusion.6 = f32[1024,4096]{1,0:T(8,128)} fusion(bf16[1024,1024]{1,0:T(8,128)(2,1)} %all-gather.5.cloned.1.call-done, bf16[1024,4096]{1,0:T(8,128)(2,1)} %param.5), kind=kOutput, calls=%fused_computation.11 | convolution fusion | flops 8589934592 | bytes 27262976 | tf_op jit(solution)/shard_map/dot_general | solution.py:20
  101.1 266.7 %reduce-scatter.11.cloned.1.call-done = f32[256,4096]{1,0:T(8,128)} async-done(((f32[1024,4096]{1,0:T(8,128)}), f32[256,4096]{1,0:T(8,128)}) %reduce-scatter.11.cloned.1.call-update) | async-done | bytes 4194320 | tf_op jit(solution)/shard_map/reduce_scatter | solution.py:31
  367.8 283.4 %reduce-scatter.7.cloned.1.call-done = f32[256,4096]{1,0:T(8,128)} async-done(((f32[1024,4096]{1,0:T(8,128)}), f32[256,4096]{1,0:T(8,128)}) %reduce-scatter.7.cloned.1.call-update) | async-done | bytes 4194320 | tf_op jit(solution)/shard_map/reduce_scatter | solution.py:28
  651.2 5.7 fusion.5
  657.6 149.9 %all-gather.7.cloned.1.call-done = bf16[1024,4096]{1,0:T(8,128)(2,1)} async-done(((bf16[256,4096]{1,0:T(8,128)(2,1)}), bf16[1024,4096]{1,0:T(8,128)(2,1)}) %all-gather.7.cloned.1.call-update) | async-done | bytes 8388624 | tf_op jit(solution)/shard_map/all_gather | solution.py:30
  807.5 15.0 %fusion.7 = f32[1024,1024]{1,0:T(8,128)} fusion(bf16[1024,4096]{1,0:T(8,128)(2,1)} %all-gather.7.cloned.1.call-done, bf16[4096,1024]{1,0:T(8,128)(2,1)} %param.6), kind=kOutput, calls=%fused_computation.12 | convolution fusion | flops 8589934592 | bytes 20971520 | tf_op jit(solution)/shard_map/dot_general | solution.py:20
  822.7 134.7 %all-gather.11.cloned.1.call-done = bf16[1024,4096]{1,0:T(8,128)(2,1)} async-done(((bf16[256,4096]{1,0:T(8,128)(2,1)}), bf16[1024,4096]{1,0:T(8,128)(2,1)}) %all-gather.11.cloned.1.call-update) | async-done | bytes 8388624 | tf_op jit(solution)/shard_map/all_gather | solution.py:35
  957.4 15.0 %fusion.9 = f32[1024,1024]{1,0:T(8,128)} fusion(bf16[1024,4096]{1,0:T(8,128)(2,1)} %all-gather.11.cloned.1.call-done, bf16[1024,4096]{1,0:T(8,128)(2,1)} %param.5), kind=kOutput, calls=%fused_computation.14 | convolution fusion | flops 8589934592 | bytes 20971520 | tf_op jit(solution)/shard_map/dot_general | solution.py:17
  972.5 1.5 copy-done.1
  974.0 14.8 %convolution_bitcast_fusion.1 = f32[1024,1,4096]{0,2,1:T(8,128)} fusion(bf16[1024,4096]{1,0:T(8,128)(2,1)} %all-gather.11.cloned.1.call-done, bf16[1024,1024]{1,0:T(8,128)(2,1)S(1)} %copy-done.1), kind=kOutput, calls=%fused_computation.1 | convolution fusion | flops 8589934592 | bytes 27262976 | tf_op jit(solution)/shard_map/dot_general | solution.py:36
  989.1 1.3 copy-done
  990.4 14.7 %convolution_bitcast_fusion = f32[1,4096,1024]{2,1,0:T(8,128)} fusion(bf16[1024,4096]{1,0:T(8,128)(2,1)} %all-gather.7.cloned.1.call-done, bf16[1024,1024]{1,0:T(8,128)(2,1)S(1)} %copy-done), kind=kOutput, calls=%fused_computation | convolution fusion | flops 8589934592 | bytes 27262976 | tf_op jit(solution)/shard_map/dot_general | solution.py:39
  1005.1 6.7 reduce-scatter.9.cloned.1.call-done
  1011.8 2.1 convert_element_type.19
  1013.9 54.5 %reduce-scatter.13.cloned.1.call-done = f32[256,1024]{1,0:T(8,128)} async-done(((f32[1024,1024]{1,0:T(8,128)}), f32[256,1024]{1,0:T(8,128)}) %reduce-scatter.13.cloned.1.call-update) | async-done | bytes 1048592 | tf_op jit(solution)/shard_map/reduce_scatter | solution.py:47
  1068.4 2.1 convert_element_type.21
  1070.5 26.5 %reduce-scatter.15.cloned.1.call-done = f32[1024,1,2048]{0,2,1:T(8,128)} async-done(((f32[1024,1,4096]{0,2,1:T(8,128)}), f32[1024,1,2048]{0,2,1:T(8,128)}) %reduce-scatter.15.cloned.1.call-update) | async-done | bytes 8388624 | tf_op jit(solution)/shard_map/reduce_scatter | solution.py:51
  1097.0 6.1 convert_element_type.22
  1103.0 6.4 copy.8
  1109.5 17.3 %reduce-scatter.17.cloned.1.call-done = f32[1,2048,1024]{2,1,0:T(8,128)} async-done(((f32[1,4096,1024]{2,1,0:T(8,128)}), f32[1,2048,1024]{2,1,0:T(8,128)}) %reduce-scatter.17.cloned.1.call-update) | async-done | bytes 8388624 | tf_op jit(solution)/shard_map/reduce_scatter | solution.py:52
  1126.8 6.1 convert_element_type.23
  (22 shorter events, 2.8 us)
Async XLA Ops:
  7.2 40.7 %all-gather.9.cloned.1.call-start = ((), (), s32[]{:S(2)}) async-start(), calls=%async_computation.10 | async-start | bytes 2621440 | tf_op jit(solution)/shard_map/all_gather | solution.py:26
  7.9 77.2 %all-gather.5.cloned.1.call-start = ((), (), s32[]{:S(2)}) async-start(), calls=%async_computation.6 | async-start | bytes 2621440 | tf_op jit(solution)/shard_map/all_gather | solution.py:25
  8.6 359.1 %reduce-scatter.11.cloned.1.call-start = ((), (), s32[]{:S(2)}) async-start(), calls=%async_computation.11 | async-start | bytes 20971520 | tf_op jit(solution)/shard_map/reduce_scatter | solution.py:31
  64.0 587.2 %reduce-scatter.7.cloned.1.call-start = ((), (), s32[]{:S(2)}) async-start(), calls=%async_computation.7 | async-start | bytes 20971520 | tf_op jit(solution)/shard_map/reduce_scatter | solution.py:28
  101.1 706.4 %all-gather.7.cloned.1.call-start = ((), (), s32[]{:S(2)}) async-start(), calls=%async_computation.8 | async-start | bytes 10485760 | tf_op jit(solution)/shard_map/all_gather | solution.py:30
  656.9 300.4 %all-gather.11.cloned.1.call-start = ((), (), s32[]{:S(2)}) async-start(), calls=%async_computation.12 | async-start | bytes 10485760 | tf_op jit(solution)/shard_map/all_gather | solution.py:35
  657.5 354.3 %reduce-scatter.9.cloned.1.call-start = ((), (), s32[]{:S(2)}) async-start(), calls=%async_computation.9 | async-start | bytes 5242880 | tf_op jit(solution)/shard_map/reduce_scatter | solution.py:44
  822.4 246.0 %reduce-scatter.13.cloned.1.call-start = ((), (), s32[]{:S(2)}) async-start(), calls=%async_computation.13 | async-start | bytes 5242880 | tf_op jit(solution)/shard_map/reduce_scatter | solution.py:47
  972.4 1.6 copy-start.1
  972.4 124.6 %reduce-scatter.15.cloned.1.call-start = ((), (), s32[]{:S(2)}) async-start(), calls=%async_computation.14 | async-start | bytes 25165824 | tf_op jit(solution)/shard_map/reduce_scatter | solution.py:51
  988.8 1.6 copy-start
  988.9 137.9 %reduce-scatter.17.cloned.1.call-start = ((), (), s32[]{:S(2)}) async-start(), calls=%async_computation.15 | async-start | bytes 25165824 | tf_op jit(solution)/shard_map/reduce_scatter | solution.py:52
Sparse Core Ops, SparseCore 0:
  9.8 38.0 all-gather.8
  49.7 35.2 all-gather.4
  87.4 280.2 reduce-scatter.10
  370.1 281.0 reduce-scatter.6
  657.1 150.3 all-gather.6
  809.5 147.8 all-gather.10
  960.9 50.9 reduce-scatter.8
  1015.6 52.6 reduce-scatter.12
  1070.7 26.2 reduce-scatter.14
  1099.2 27.5 reduce-scatter.16
where the time goes:
time: 1140 us
  waiting for transfers between devices  1000 us (88%)
  matrix products  91.5 us (8%)
  other arithmetic  22.1 us (2%)
  between operations  14.2 us (1%)
    reduce_scatter x1, waiting for transfers between devices, on_device(): lax.psum_scatter(rows_times(x_full, w_in, False), 'row', scatter_dimensio...  283 us
    reduce_scatter x1, waiting for transfers between devices, on_device(): lax.psum_scatter(rows_times(grad_full, w_out, True), 'row', scatter_dimen...  267 us
    all_gather x1, waiting for transfers between devices, on_device(): lax.all_gather(act_value.astype(jnp.bfloat16), 'row', axis=0, tiled=True)  150 us
    all_gather x1, waiting for transfers between devices, on_device(): pre_grad_full = lax.all_gather(pre_grad, 'row', axis=0, tiled=True)  135 us
    reduce_scatter x1, waiting for transfers between devices, on_device(): lax.psum_scatter(rows_times(pre_grad_full, w_in, True), 'col', scatter_di...  54.5 us
    all_gather x1, waiting for transfers between devices, on_device(): lax.all_gather(out_grad, 'col', axis=0, tiled=True)  39.2 us
    dot_general x2, matrix products, rows_times(): lax.dot_general(left, right, (((1,), (1,)), ((), ())), preferred_element_...  31.1 us
    dot_general x2, matrix products, rows_times(): return jnp.dot(left, right, preferred_element_type=jnp.float32)  30.9 us
  transfers between devices with their start and end apart: 10, of which 10 were waited for; matrix products, arithmetic and copies ran while one was open for 9% of the time, Pallas kernels for 0%

commit v1 on v0

v1 whole, which is shorter than its diff:
```python
import functools
import math

import jax
import jax.numpy as jnp
from jax import lax
from jax.experimental import pallas as pl
from jax.experimental.pallas import tpu as pltpu
from jax.sharding import PartitionSpec as P

ROWS = 128
VMEM_MIB = 64
PARTIAL = jnp.bfloat16
ANY = pl.BlockSpec(memory_space=pltpu.HBM)
SMALL = pl.CostEstimate(flops=1024, bytes_accessed=1024, transcendentals=0)


def params(mib):
    return pltpu.CompilerParams(vmem_limit_bytes=mib << 20)


def hbm_out(shape, dtype=jnp.bfloat16):
    return jax.ShapeDtypeStruct(shape, dtype)


def row_chunks(rows):
    parts = 4 if rows % 64 == 0 else 1
    return [(i * (rows // parts), rows // parts) for i in range(parts)]


def across(left, right):
    return lax.dot_general(left, right, (((1,), (1,)), ((), ())), preferred_element_type=jnp.float32)


def project(streams, blocks, weights, replica, hidden, after):
    width = blocks[0][0][0].shape[1]
    tile = min(512, hidden)
    steps = hidden // tile
    operands, specs, out_specs, out_shape = [], [], [], []
    for s in streams:
        if s == 0:
            operands.append(weights[0])
            specs.append(pl.BlockSpec((width, tile), lambda i, d: (0, d[0] * steps + i)))
        else:
            operands.append(weights[1])
            specs.append(pl.BlockSpec((tile, width), lambda i, d: (d[0] * steps + i, 0)))
        for both, first, rows in blocks:
            at = first // rows
            if isinstance(both, tuple):
                operands.append(both[s])
                specs.append(pl.BlockSpec((rows, width), lambda i, d, at=at: (at, 0)))
            else:
                operands.append(both)
                specs.append(pl.BlockSpec((None, rows, width), lambda i, d, s=s, at=at: (s, at, 0)))
            out_specs.append(pl.BlockSpec((rows, tile), lambda i, d: (0, i)))
            out_shape.append(hbm_out((rows, hidden), PARTIAL))

    def body(replica_ref, *refs):
        outs = iter(refs[len(operands) + len(after) :])
        given = iter(refs)
        for s in streams:
            weight = next(given)[...]
            for _ in blocks:
                x = next(given)[...]
                out = next(outs)
                if s == 0:
                    value = jnp.dot(x, weight, preferred_element_type=jnp.float32)
                else:
                    value = across(x, weight)
                out[...] = value.astype(out.dtype)

    done = pl.pallas_call(
        body,
        grid_spec=pltpu.PrefetchScalarGridSpec(
            num_scalar_prefetch=1,
            grid=(steps,),
            in_specs=specs + [ANY] * len(after),
            out_specs=out_specs,
        ),
        out_shape=out_shape,
        compiler_params=params(VMEM_MIB),
        cost_estimate=SMALL,
        name="project",
    )(replica, *operands, *after)
    return [done[i : i + len(blocks)] for i in range(0, len(done), len(blocks))]


def hold(array, after):
    return pl.pallas_call(
        lambda *refs: None,
        in_specs=[ANY] * (1 + len(after)),
        out_specs=ANY,
        out_shape=hbm_out(array.shape, array.dtype),
        input_output_aliases={0: 0},
        compiler_params=params(VMEM_MIB),
        cost_estimate=SMALL,
        name="hold",
    )(array, *after)


def pack(pair, after):
    def body(*refs):
        out, held, in_sem, out_sem = refs[-4:]
        into = [pltpu.make_async_copy(refs[i], held.at[i], in_sem.at[i]) for i in range(2)]
        out_of = [pltpu.make_async_copy(held.at[i], out.at[i], out_sem.at[i]) for i in range(2)]
        for copy in into:
            copy.start()
        for i in range(2):
            into[i].wait()
            out_of[i].start()
        for copy in out_of:
            copy.wait()

    return pl.pallas_call(
        body,
        in_specs=[ANY] * (2 + len(after)),
        out_specs=ANY,
        out_shape=hbm_out((2, *pair[0].shape), pair[0].dtype),
        scratch_shapes=[
            pltpu.VMEM((2, *pair[0].shape), pair[0].dtype),
            pltpu.SemaphoreType.DMA((2,)),
            pltpu.SemaphoreType.DMA((2,)),
        ],
        compiler_params=params(VMEM_MIB),
        cost_estimate=SMALL,
        name="pack",
    )(*pair, *after)


def own_place(ring, line):
    row = lax.axis_index("row")
    return jnp.where(lax.axis_index("dp") == ring, row, line - 1 - row)


def apart(after, arrays):
    return [a for a in after if all(a is not b for b in arrays)]


def distinct(arrays):
    found = []
    for array in arrays:
        if all(array is not seen for seen in found):
            found.append(array)
    return found, [next(i for i, seen in enumerate(found) if seen is a) for a in arrays]


def chain_step(ring, got, partials, after):
    _, rows, hidden = got.shape
    late = len(partials)
    chunks = row_chunks(rows)
    arrays, which = distinct([array for part in partials for array in part[:2]])

    def body(*refs):
        got_h, terms = refs[0], refs[1 : 1 + len(arrays)]
        out_h = refs[1 + len(arrays) + len(after)]
        got_v, own_v, out_v, got_sem, own_sem, out_sem = refs[-6:]
        place = own_place(ring, late)
        copies = []
        for s in range(2):
            for c, (first, count) in enumerate(chunks):
                part = pl.ds(first, count)

                def own_copy(j, s=s, c=c, first=first, count=count, part=part):
                    return pltpu.make_async_copy(
                        terms[which[2 * j + s]].at[pl.ds(partials[j][2] + first, count)],
                        own_v.at[s, part],
                        own_sem.at[s, c],
                    )

                got_copy = pltpu.make_async_copy(
                    got_h.at[s, part], got_v.at[s, part], got_sem.at[s, c]
                )
                out_copy = pltpu.make_async_copy(
                    out_v.at[s, part], out_h.at[s, part], out_sem.at[s, c]
                )
                copies.append((s, part, got_copy, own_copy(0), out_copy))
                got_copy.start()
                for j in range(late):

                    @pl.when(place == j)
                    def _(j=j, own_copy=own_copy):
                        own_copy(j).start()

        for s, part, got_copy, own_copy, out_copy in copies:
            got_copy.wait()
            own_copy.wait()

            @pl.when(place == 0)
            def _(s=s, part=part):
                out_v[s, part] = own_v[s, part].astype(out_v.dtype)

            @pl.when(place != 0)
            def _(s=s, part=part):
                out_v[s, part] = (
                    got_v[s, part].astype(jnp.float32) + own_v[s, part].astype(jnp.float32)
                ).astype(out_v.dtype)

            out_copy.start()
        for copy in copies:
            copy[-1].wait()

    return pl.pallas_call(
        body,
        in_specs=[ANY] * (1 + len(arrays) + len(after)),
        out_specs=ANY,
        out_shape=hbm_out((2, rows, hidden)),
        scratch_shapes=[
            pltpu.VMEM((2, rows, hidden), jnp.bfloat16),
            pltpu.VMEM((2, rows, hidden), PARTIAL),
            pltpu.VMEM((2, rows, hidden), jnp.bfloat16),
        ]
        + [pltpu.SemaphoreType.DMA((2, len(chunks)))] * 3,
        compiler_params=params(VMEM_MIB),
        cost_estimate=SMALL,
        name="chain_step",
    )(got, *arrays, *after)


def activate(partial, got, kept, kept_rows, kept_row, after):
    _, rows, hidden = got[0][0].shape
    line = len(got[0]) + 1
    after = apart(after, kept)
    given, which = distinct([*partial[:2], *got[0], *got[1]])
    step_rows, step_cols = 16, min(512, hidden)
    halves = 2 if rows % 32 == 0 else 1
    part_rows = rows // halves
    across_cols = hidden // step_cols
    tiles = (part_rows // step_rows) * across_cols

    def body(*refs):
        terms = refs[: len(given)]
        outs = refs[len(given) + len(kept) + len(after) :][:2]
        own_v, got_v, out_v, own_sem, got_sem, out_sem = refs[-6:]

        def own_copy(s, h):
            part = pl.ds(h * part_rows, part_rows)
            return pltpu.make_async_copy(
                terms[which[s]].at[pl.ds(partial[2] + h * part_rows, part_rows)],
                own_v.at[s, part],
                own_sem.at[s, h],
            )

        def got_copy(ring, j, s, h):
            part = pl.ds(h * part_rows, part_rows)
            return pltpu.make_async_copy(
                terms[which[2 + ring * (line - 1) + j]].at[s, part],
                got_v.at[ring, s, part],
                got_sem.at[ring, s, h],
            )

        for h in range(halves):
            for s in range(2):
                own_copy(s, h).start()
                for ring in range(2):
                    place = own_place(ring, line)

                    @pl.when(place == 0)
                    def _(ring=ring, s=s, h=h):
                        part = pl.ds(h * part_rows, part_rows)
                        got_v[ring, s, part] = jnp.zeros((part_rows, hidden), got_v.dtype)

                    for j in range(1, line):

                        @pl.when(place == j)
                        def _(ring=ring, j=j, s=s, h=h):
                            got_copy(ring, j - 1, s, h).start()

        out_copies = []
        for h in range(halves):
            for s in range(2):
                own_copy(s, h).wait()
                for ring in range(2):

                    @pl.when(own_place(ring, line) != 0)
                    def _(ring=ring, s=s, h=h):
                        got_copy(ring, 0, s, h).wait()

            def tile(i, _, h=h):
                at = pl.multiple_of((i // across_cols) * step_rows, step_rows)
                r = pl.ds(h * part_rows + at, step_rows)
                c = pl.ds(pl.multiple_of((i % across_cols) * step_cols, step_cols), step_cols)
                pre, grad = (
                    own_v[s, r, c].astype(jnp.float32)
                    + got_v[0, s, r, c].astype(jnp.float32)
                    + got_v[1, s, r, c].astype(jnp.float32)
                    for s in range(2)
                )
                cdf = 0.5 * (1.0 + lax.erf(pre * (1.0 / math.sqrt(2.0))))
                pdf = jnp.exp(-0.5 * pre * pre) * (1.0 / math.sqrt(2.0 * math.pi))
                out_v[0, r, c] = (pre * cdf).astype(jnp.bfloat16)
                out_v[1, r, c] = (grad * (cdf + pre * pdf)).astype(jnp.bfloat16)
                return 0

            lax.fori_loop(0, tiles, tile, 0)
            for i in range(2):
                copy = pltpu.make_async_copy(
                    out_v.at[i, pl.ds(h * part_rows, part_rows)],
                    outs[i].at[pl.ds(kept_row + h * part_rows, part_rows)],
                    out_sem.at[i, h],
                )
                copy.start()
                out_copies.append(copy)
        for copy in out_copies:
            copy.wait()

    return pl.pallas_call(
        body,
        in_specs=[ANY] * (len(given) + len(kept) + len(after)),
        out_specs=[ANY] * 2,
        out_shape=[hbm_out((kept_rows, hidden))] * 2,
        input_output_aliases={len(given) + i: i for i in range(len(kept))},
        scratch_shapes=[
            pltpu.VMEM((2, rows, hidden), PARTIAL),
            pltpu.VMEM((2, 2, rows, hidden), jnp.bfloat16),
            pltpu.VMEM((2, rows, hidden), jnp.bfloat16),
            pltpu.SemaphoreType.DMA((2, halves)),
            pltpu.SemaphoreType.DMA((2, 2, halves)),
            pltpu.SemaphoreType.DMA((2, halves)),
        ],
        compiler_params=params(VMEM_MIB),
        cost_estimate=SMALL,
        name="activate",
    )(*given, *kept, *after)


def share_of(stream, hid, first, rows, weight, after):
    hidden = hid.shape[1]
    width = weight.shape[1 - stream]
    parts = 4 if width % 512 == 0 else 1
    cols = width // parts

    def body(*refs):
        hid_h, weight_h = refs[:2]
        out_h = refs[2 + len(after)]
        hid_v, weight_v, out_v, hid_sem, weight_sem, out_sem = refs[-6:]
        mine = pl.ds(pl.multiple_of(lax.axis_index("dp") * hidden, hidden), hidden)
        hid_copy = pltpu.make_async_copy(hid_h.at[pl.ds(first, rows)], hid_v, hid_sem)
        hid_copy.start()
        weight_copies, out_copies = [], []
        for i in range(parts):
            part = pl.ds(i * cols, cols)
            source = weight_h.at[mine, part] if stream == 0 else weight_h.at[part, mine]
            weight_copies.append(
                pltpu.make_async_copy(source, weight_v.at[i], weight_sem.at[i])
            )
            weight_copies[-1].start()
            out_copies.append(
                pltpu.make_async_copy(out_v.at[:, part], out_h.at[:, part], out_sem.at[i])
            )
        hid_copy.wait()
        for i in range(parts):
            weight_copies[i].wait()
            part = slice(i * cols, (i + 1) * cols)
            if stream == 0:
                out_v[:, part] = jnp.dot(
                    hid_v[...], weight_v[i], preferred_element_type=jnp.float32
                )
            else:
                out_v[:, part] = across(hid_v[...], weight_v[i])
            out_copies[i].start()
        for copy in out_copies:
            copy.wait()

    return pl.pallas_call(
        body,
        in_specs=[ANY] * (2 + len(after)),
        out_specs=ANY,
        out_shape=hbm_out((rows, width), jnp.float32),
        scratch_shapes=[
            pltpu.VMEM((rows, hidden), jnp.bfloat16),
            pltpu.VMEM((parts, hidden, cols) if stream == 0 else (parts, cols, hidden), jnp.bfloat16),
            pltpu.VMEM((rows, width), jnp.float32),
            pltpu.SemaphoreType.DMA(()),
            pltpu.SemaphoreType.DMA((parts,)),
            pltpu.SemaphoreType.DMA((parts,)),
        ],
        compiler_params=params(VMEM_MIB),
        cost_estimate=SMALL,
        name="share_of",
    )(hid, weight, *after)


def on_device(line, cols, tokens, w_in, w_out, out_grad):
    block, width = tokens.shape
    hidden = w_in.shape[1] // 2
    rows = min(ROWS, block)
    per = block // rows
    replica = lax.axis_index("dp").astype(jnp.int32).reshape(1)

    def ring_pairs(ring):
        up, down = ring * line, (1 - ring) * line
        pairs = [(up + i, up + i + 1) for i in range(line - 1)]
        pairs += [(down + i + 1, down + i) for i in range(line - 1)]
        return [*pairs, (up + line - 1, down + line - 1), (down, up)]

    def over_dp(x):
        return lax.ppermute(x, "dp", [(0, 1), (1, 0)])

    def over_col(x, k):
        return lax.ppermute(x, "col", [(i, i ^ k) for i in range(cols)])

    order = [(0, 0)] + [(d, k) for k in range(1, cols) for d in range(2)] + [(1, 0)]
    final = len(order) - 1
    count = len(order) * per
    ends = [count - count // 4, count]
    starts = [0, *ends[:-1]]

    last = []
    xg = {}
    partial = {}
    came = [[], []]
    kept = [()] * len(ends)
    shares = {}
    sums = [None, None]
    collected = {}

    def project_blocks(streams, parts):
        nonlocal last
        blocks = [part[1:] for part in parts]
        done = project(streams, blocks, (w_in, w_out), replica, hidden, last)
        for s, arrays in zip(streams, done, strict=True):
            for (b, _, _, n), array in zip(parts, arrays, strict=True):
                for i in range(n // rows):
                    partial.setdefault(b + i, [None, None, i * rows])[s] = array
        last = [done[-1][-1]]

    def project_one(r):
        project_blocks((0, 1), [(r * per, xg[order[r]], 0, block)])

    def step(ring, t):
        nonlocal last
        if t == 0:
            send = pack(partial[0][:2], last)
        else:
            terms = [partial[min(max(t - j, 0), count - 1)] for j in range(line)]
            send = chain_step(ring, came[ring][t - 1], terms, last)
        last = [send]
        came[ring].append(lax.ppermute(send, ("dp", "row"), ring_pairs(ring)))

    def gather_own():
        nonlocal last
        xg[0, 0] = pack((tokens, out_grad), last)
        last = [xg[0, 0]]
        for k in range(1, cols):
            if k & -k == k:
                xg[0, k] = over_col(xg[0, 0], k)
        xg[1, 0] = over_dp(xg[0, 0])

    def spread(k):
        nonlocal last
        xg[0, k] = hold(xg[0, k], last)
        last = [xg[0, k]]
        xg[1, k] = over_dp(xg[0, k])
        low = k & -k
        for j in range(1, low):
            if j & -j == j:
                xg[0, k | j] = over_col(xg[0, k], j)

    def activate_block(b):
        nonlocal last
        g = next(i for i, end in enumerate(ends) if b < end)
        got = [[came[ring][b + j] for j in range(line - 1)] for ring in range(2)]
        kept[g] = activate(
            partial[b],
            got,
            kept[g],
            (ends[g] - starts[g]) * rows,
            (b - starts[g]) * rows,
            last,
        )
        last = [kept[g][0]]

    def share_block(stream, r):
        nonlocal last
        b = r * per
        g = next(i for i, end in enumerate(ends) if b < end)
        shares[stream, r] = share_of(
            stream, kept[g][stream], (b - starts[g]) * rows, block, (w_out, w_in)[stream], last
        )
        last = [shares[stream, r]]

    def add_group(g, which):
        nonlocal last
        parts, b = [], starts[g]
        while b < ends[g]:
            until = min(ends[g], (b // per + 1) * per)
            part = xg[order[b // per]][which]
            parts.append(part[(b % per) * rows : (b % per + until - b) * rows])
            b = until
        outer = jnp.concatenate(parts) if len(parts) > 1 else parts[0]
        hid = kept[g][1 - which]
        sides = (outer, hid) if which == 0 else (hid, outer)
        term = lax.dot_general(*sides, (((0,), (0,)), ((), ())), preferred_element_type=jnp.float32)
        sums[which] = term if sums[which] is None else sums[which] + term
        last = [*last, sums[which]]

    def pair_sum(stream, k):
        nonlocal last
        both = shares[stream, 2 * k - 1] + over_dp(shares[stream, 2 * k])
        both = both.astype(jnp.bfloat16)
        last = [*last, both]
        collected[stream, k] = over_col(both, k)

    todo = {}

    def at(t, window, *what):
        todo.setdefault((t, window), []).append(what)

    own = (tokens, out_grad)
    at(0, 0, gather_own)
    if per > 1:
        at(0, 1, project_blocks, (0, 1), [(i, own, i * rows, rows) for i in range(1, per)])
    at(1, 0, project_one, final)
    for r in range(1, final):
        d, k = order[r]
        if cols <= 4:
            when, spread_when = r + 2, max(2 * k, 2)
        else:
            when, spread_when = 2 * r - 1, 2 * r - 2
        if d == 0 and k < 3:
            at(*divmod(spread_when, 2), spread, k)
        at(*divmod(when, 2), project_one, r)
        if d == 0 and k >= 3:
            at(*divmod(spread_when, 2), spread, k)
    for b in range(count):
        if b < count - 2:
            at(b + line, 0, activate_block, b)
        elif b == count - 2:
            at(b + line - 1, 1, activate_block, b)
    for r in range(final):
        t = (r + 1) * per - 1 + line
        early = t + 1 < count + line - 2
        for stream in range(2):
            when = t + stream if early else t
            at(when, 1, share_block, stream, r)
            if order[r][0] == 1:
                k = order[r][1]
                at(when + 1 if early else t, 1, pair_sum, stream, k)
                at(when + 2, 1, lambda stream=stream, k=k: last.append(collected[stream, k]))
    at(ends[0] + line, 0, add_group, 0, 0)
    at(ends[0] + line + 1, 0, add_group, 0, 1)

    def run(t, window):
        for what, *rest in todo.pop((t, window), []):
            what(*rest)

    project_blocks((0, 1), [(0, (tokens, out_grad), 0, rows)])
    for t in range(count + line - 2):
        for ring in range(2):
            step(ring, t)
            run(t, ring)
    for t, window in sorted(todo):
        run(t, window)
    activate_block(count - 1)
    results = []
    for stream in range(2):
        share_block(stream, final)
    add_group(len(ends) - 1, 0)
    add_group(len(ends) - 1, 1)

    for stream in range(2):
        total = shares[stream, 0]
        for k in range(1, cols):
            total = total + collected[stream, k].astype(jnp.float32)
        results.append((total + over_dp(shares[stream, final])).astype(jnp.bfloat16))
    grad_w_in, grad_w_out = (s.astype(jnp.bfloat16) for s in sums)
    return (*results, grad_w_in[:, None, :], grad_w_out[None])


def solution(mesh):
    placed = (P(("dp", "col"), "row"), P("row", "col"), P("col", "row"), P(("dp", "col"), "row"))
    return jax.shard_map(
        functools.partial(on_device, mesh.shape["row"], mesh.shape["col"]),
        mesh=mesh,
        in_specs=placed,
        out_specs=(
            P(("dp", "col"), "row"),
            P(("dp", "col"), "row"),
            P("row", "col", "dp"),
            P("col", "dp", "row"),
        ),
        check_vma=False,
    )
```

time: 1140 us -> 560 us (0.49)
  waiting for transfers between devices: 1000 us -> 107 us
  Pallas kernels: 0 us -> 290 us
  starting transfers between devices: 0.8 us -> 72.4 us
  matrix products: 91.5 us -> 40.4 us
  between operations: 14.2 us -> 1.96 us
    reduce_scatter x6 -> x0, waiting for transfers between devices: 655 us -> none  [the longest x1 283 us: on_device(): lax.psum_scatter(rows_times(x_full, w_in, False), 'row', scatter_dimensio...]
    all_gather x4 -> x0, waiting for transfers between devices: 345 us -> none  [the longest x1 150 us: on_device(): lax.all_gather(act_value.astype(jnp.bfloat16), 'row', axis=0, tiled=True)]
    pallas_call x0 -> x81, Pallas kernels: none -> 290 us  [the longest x34 85.7 us: chain_step(): pl.pallas_call(body, in_specs=[ANY] * (1 + len(arrays) + len(after)), out...]
    ppermute x0 -> x57, waiting for transfers between devices: none -> 107 us  [the longest x36 78.8 us: step(): came[ring].append(lax.ppermute(send, ('dp', 'row'), ring_pairs(ring)))]
    ppermute x0 -> x57, starting transfers between devices: none -> 72.4 us  [the longest x36 54 us: step(): came[ring].append(lax.ppermute(send, ('dp', 'row'), ring_pairs(ring)))]
    dot_general x6 -> x4, matrix products: 91.5 us -> 40.4 us  [add_group(): lax.dot_general(*sides, (((0,), (0,)), ((), ())), preferred_element_type=...]
  transfers between devices with their start and end apart: 10 -> 57, of which waited for: 10 -> 21; matrix products, arithmetic and copies ran while one was open for 9% -> 13% of each run, Pallas kernels for 0% -> 47%
where the time goes in v1:
time: 560 us; the launch traced here: 549 us
  Pallas kernels  290 us (52%)
  waiting for transfers between devices  107 us (19%)
  starting transfers between devices  72.4 us (13%)
  matrix products  40.4 us (7%)
  other arithmetic  18.9 us (3%)
  local copies, waits for them, and re-layouts  18.7 us (3%)
    pallas_call x34, Pallas kernels, chain_step(): pl.pallas_call(body, in_specs=[ANY] * (1 + len(arrays) + len(after)), out...  85.7 us
    pallas_call x16, Pallas kernels, share_of(): pl.pallas_call(body, in_specs=[ANY] * (2 + len(after)), out_specs=ANY, ou...  83 us
    ppermute x36, waiting for transfers between devices, step(): came[ring].append(lax.ppermute(send, ('dp', 'row'), ring_pairs(ring)))  78.8 us
    pallas_call x9, Pallas kernels, project(): pl.pallas_call(body, grid_spec=pltpu.PrefetchScalarGridSpec(num_scalar_pr...  58.6 us
    pallas_call x16, Pallas kernels, activate(): pl.pallas_call(body, in_specs=[ANY] * (len(given) + len(kept) + len(after...  56 us
    ppermute x36, starting transfers between devices, step(): came[ring].append(lax.ppermute(send, ('dp', 'row'), ring_pairs(ring)))  54 us
    dot_general x4, matrix products, add_group(): lax.dot_general(*sides, (((0,), (0,)), ((), ())), preferred_element_type=...  40.4 us
    ppermute x9, waiting for transfers between devices, over_col(): return lax.ppermute(x, 'col', [(i, i ^ k) for i in range(cols)])  26 us
  transfers between devices with their start and end apart: 57, of which 21 were waited for; matrix products, arithmetic and copies ran while one was open for 13% of the time, Pallas kernels for 47%

profile of v1, /device:TPU:0, one launch (start us, length us, event | category | flops | bytes accessed | tf_op | source)
XLA Modules:
  0.0 549.3 jit_solution(17684414804646587319)
XLA Ops:
  0.6 6.1 %project.9 = (bf16[128,2048]{1,0:T(8,128)(2,1)}, bf16[128,2048]{1,0:T(8,128)(2,1)}) custom-call(s32[1]{0:T(128)} %bitcast.replica_ref, bf16[1024,4096]{1,0:T(8,128)(2,1)} %refs_1_.37, bf16[256,1024]{1,0:T(8,128)(2,1)} %refs_1_.21, bf16[4096,1024]{1,0:T(8,128)(2,1)} %refs_1_.36, bf16[256,1024]{1,0:T(8,128)(2,1)} %refs_3_.3), custom_call_target="tpu_custom_call" | custom-call | flops 1024 | bytes 1024 | tf_op jit(solution)/shard_map/project/pallas_call | solution.py:72
  17.8 6.1 %project.10 = (bf16[128,2048]{1,0:T(8,128)(2,1)}, bf16[128,2048]{1,0:T(8,128)(2,1)}) custom-call(s32[1]{0:T(128)} %bitcast.replica_ref, bf16[1024,4096]{1,0:T(8,128)(2,1)} %refs_1_.37, bf16[256,1024]{1,0:T(8,128)(2,1)} %refs_1_.21, bf16[4096,1024]{1,0:T(8,128)(2,1)} %refs_1_.36, bf16[256,1024]{1,0:T(8,128)(2,1)} %refs_3_.3, bf16[2,128,2048]{2,1,0:T(8,128)(2,1)} %pack.5.refs_4_), custom_call_target="tpu_custom_call" | custom-call | flops 1024 | bytes 1024 | tf_op jit(solution)/shard_map/project/pallas_call | solution.py:72
  34.1 6.6 %project.11 = (bf16[256,2048]{1,0:T(8,128)(2,1)}, bf16[256,2048]{1,0:T(8,128)(2,1)}) custom-call(s32[1]{0:T(128)} %bitcast.replica_ref, bf16[1024,4096]{1,0:T(8,128)(2,1)} %refs_1_.37, bf16[2,256,1024]{2,1,0:T(8,128)(2,1)} %collective-permute-done.3.refs_1_.refs_3_, bf16[4096,1024]{1,0:T(8,128)(2,1)} %refs_1_.36, ...), custom_call_target="tpu_custom_call" | custom-call | flops 1024 | bytes 1024 | tf_op jit(solution)/shard_map/project/pallas_call | solution.py:72
  45.1 6.6 %project.12 = (bf16[256,2048]{1,0:T(8,128)(2,1)}, bf16[256,2048]{1,0:T(8,128)(2,1)}) custom-call(s32[1]{0:T(128)} %bitcast.replica_ref, bf16[1024,4096]{1,0:T(8,128)(2,1)} %refs_1_.37, bf16[2,256,1024]{2,1,0:T(8,128)(2,1)} %hold.3.refs_5_.refs_1_.refs_3_, bf16[4096,1024]{1,0:T(8,128)(2,1)} %refs_1_.36, bf16[2,256,1024]{2,1,0:T(8,128)(2,1)} %hold.3.refs_5_.refs_1_.refs_3_, ...), custom_call_target="tpu_custom_call" | custom-call | flops 1024 | bytes 1024 | tf_op jit(solution)/shard_map/project/pallas_call | solution.py:72
  56.1 6.6 %project.13 = (bf16[256,2048]{1,0:T(8,128)(2,1)}, bf16[256,2048]{1,0:T(8,128)(2,1)}) custom-call(s32[1]{0:T(128)} %bitcast.replica_ref, bf16[1024,4096]{1,0:T(8,128)(2,1)} %refs_1_.37, bf16[2,256,1024]{2,1,0:T(8,128)(2,1)} %collective-permute-done.7.refs_1_.refs_3_, bf16[4096,1024]{1,0:T(8,128)(2,1)} %refs_1_.36, ...), custom_call_target="tpu_custom_call" | custom-call | flops 1024 | bytes 1024 | tf_op jit(solution)/shard_map/project/pallas_call | solution.py:72
  71.9 6.6 %project.14 = (bf16[256,2048]{1,0:T(8,128)(2,1)}, bf16[256,2048]{1,0:T(8,128)(2,1)}) custom-call(s32[1]{0:T(128)} %bitcast.replica_ref, bf16[1024,4096]{1,0:T(8,128)(2,1)} %refs_1_.37, bf16[2,256,1024]{2,1,0:T(8,128)(2,1)} %hold.4.refs_7_.refs_1_.refs_3_, bf16[4096,1024]{1,0:T(8,128)(2,1)} %refs_1_.36, bf16[2,256,1024]{2,1,0:T(8,128)(2,1)} %hold.4.refs_7_.refs_1_.refs_3_, ...), custom_call_target="tpu_custom_call" | custom-call | flops 1024 | bytes 1024 | tf_op jit(solution)/shard_map/project/pallas_call | solution.py:72
  82.8 6.6 %project.15 = (bf16[256,2048]{1,0:T(8,128)(2,1)}, bf16[256,2048]{1,0:T(8,128)(2,1)}) custom-call(s32[1]{0:T(128)} %bitcast.replica_ref, bf16[1024,4096]{1,0:T(8,128)(2,1)} %refs_1_.37, bf16[2,256,1024]{2,1,0:T(8,128)(2,1)} %collective-permute-done.12.refs_1_.refs_3_, bf16[4096,1024]{1,0:T(8,128)(2,1)} %refs_1_.36, ...), custom_call_target="tpu_custom_call" | custom-call | flops 1024 | bytes 1024 | tf_op jit(solution)/shard_map/project/pallas_call | solution.py:72
  96.3 6.6 %project.16 = (bf16[256,2048]{1,0:T(8,128)(2,1)}, bf16[256,2048]{1,0:T(8,128)(2,1)}) custom-call(s32[1]{0:T(128)} %bitcast.replica_ref, bf16[1024,4096]{1,0:T(8,128)(2,1)} %refs_1_.37, bf16[2,256,1024]{2,1,0:T(8,128)(2,1)} %hold.5.refs_7_.refs_1_.refs_3_, bf16[4096,1024]{1,0:T(8,128)(2,1)} %refs_1_.36, bf16[2,256,1024]{2,1,0:T(8,128)(2,1)} %hold.5.refs_7_.refs_1_.refs_3_, ...), custom_call_target="tpu_custom_call" | custom-call | flops 1024 | bytes 1024 | tf_op jit(solution)/shard_map/project/pallas_call | solution.py:72
  107.0 6.6 %project.17 = (bf16[256,2048]{1,0:T(8,128)(2,1)}, bf16[256,2048]{1,0:T(8,128)(2,1)}) custom-call(s32[1]{0:T(128)} %bitcast.replica_ref, bf16[1024,4096]{1,0:T(8,128)(2,1)} %refs_1_.37, bf16[2,256,1024]{2,1,0:T(8,128)(2,1)} %collective-permute-done.14.refs_1_.refs_3_, bf16[4096,1024]{1,0:T(8,128)(2,1)} %refs_1_.36, ...), custom_call_target="tpu_custom_call" | custom-call | flops 1024 | bytes 1024 | tf_op jit(solution)/shard_map/project/pallas_call | solution.py:72
  129.7 12.9 %collective-permute-done.16.refs_0_.refs_7_.refs_6_.refs_5_ = bf16[2,128,2048]{2,1,0:T(8,128)(2,1)} collective-permute-done((bf16[2,128,2048]{2,1,0:T(8,128)(2,1)}, bf16[2,128,2048]{2,1,0:T(8,128)(2,1)}, u32[]{:S(2)}, u32[]{:S(2)}) %collective-permute-start.16) | collective-permute-done | bytes 1048608 | tf_op jit(solution)/shard_map/ppermute | solution.py:438
  158.5 6.0 %collective-permute-done.18.refs_0_.refs_7_.refs_6_.refs_5_ = bf16[2,128,2048]{2,1,0:T(8,128)(2,1)} collective-permute-done((bf16[2,128,2048]{2,1,0:T(8,128)(2,1)}, bf16[2,128,2048]{2,1,0:T(8,128)(2,1)}, u32[]{:S(2)}, u32[]{:S(2)}) %collective-permute-start.18) | collective-permute-done | bytes 1048608 | tf_op jit(solution)/shard_map/ppermute | solution.py:438
  181.9 7.6 %collective-permute-done.20.refs_0_.refs_7_.refs_6_.refs_5_ = bf16[2,128,2048]{2,1,0:T(8,128)(2,1)} collective-permute-done((bf16[2,128,2048]{2,1,0:T(8,128)(2,1)}, bf16[2,128,2048]{2,1,0:T(8,128)(2,1)}, u32[]{:S(2)}, u32[]{:S(2)}) %collective-permute-start.20) | collective-permute-done | bytes 1048608 | tf_op jit(solution)/shard_map/ppermute | solution.py:438
  208.1 7.9 %collective-permute-done.22.refs_0_.refs_7_.refs_6_.refs_5_ = bf16[2,128,2048]{2,1,0:T(8,128)(2,1)} collective-permute-done((bf16[2,128,2048]{2,1,0:T(8,128)(2,1)}, bf16[2,128,2048]{2,1,0:T(8,128)(2,1)}, u32[]{:S(2)}, u32[]{:S(2)}) %collective-permute-start.22) | collective-permute-done | bytes 1048608 | tf_op jit(solution)/shard_map/ppermute | solution.py:438
  235.8 5.6 %collective-permute-done.24.refs_0_.refs_7_.refs_6_.refs_5_ = bf16[2,128,2048]{2,1,0:T(8,128)(2,1)} collective-permute-done((bf16[2,128,2048]{2,1,0:T(8,128)(2,1)}, bf16[2,128,2048]{2,1,0:T(8,128)(2,1)}, u32[]{:S(2)}, u32[]{:S(2)}) %collective-permute-start.24) | collective-permute-done | bytes 1048608 | tf_op jit(solution)/shard_map/ppermute | solution.py:438
  268.7 5.3 share_of.21.refs_5_
  274.1 7.9 %collective-permute-done.29.refs_0_.refs_4_.refs_3_.refs_2_ = bf16[2,128,2048]{2,1,0:T(8,128)(2,1)} collective-permute-done((bf16[2,128,2048]{2,1,0:T(8,128)(2,1)}, bf16[2,128,2048]{2,1,0:T(8,128)(2,1)}, u32[]{:S(2)}, u32[]{:S(2)}) %collective-permute-start.29) | collective-permute-done | bytes 1048608 | tf_op jit(solution)/shard_map/ppermute | solution.py:438
  299.6 5.6 %collective-permute-done.26.refs_3_ = bf16[256,1024]{1,0:T(8,128)(2,1)} collective-permute-done((bf16[256,1024]{1,0:T(8,128)(2,1)}, bf16[256,1024]{1,0:T(8,128)(2,1)}, u32[]{:S(2)}, u32[]{:S(2)}) %collective-permute-start.26) | collective-permute-done | bytes 524320 | tf_op jit(solution)/shard_map/ppermute | solution.py:400
  325.2 10.2 %collective-permute-done.35.refs_3_ = bf16[256,1024]{1,0:T(8,128)(2,1)} collective-permute-done((bf16[256,1024]{1,0:T(8,128)(2,1)}, bf16[256,1024]{1,0:T(8,128)(2,1)}, u32[]{:S(2)}, u32[]{:S(2)}) %collective-permute-start.35) | collective-permute-done | bytes 524320 | tf_op jit(solution)/shard_map/ppermute | solution.py:400
  376.1 5.3 share_of.25.refs_5_
  413.6 11.8 %fusion.22.refs_6_ = f32[1024,2048]{1,0:T(8,128)} fusion(bf16[1536,1024]{1,0:T(8,128)(2,1)} %get-tuple-element.109, bf16[1536,2048]{1,0:T(8,128)(2,1)} %get-tuple-element.96.refs_0_), kind=kOutput, calls=%fused_computation.48 | convolution fusion | flops 6442450944 | bytes 17825792 | tf_op jit(solution)/shard_map/dot_general | solution.py:493
  438.1 11.8 %fusion.23.refs_4_ = f32[2048,1024]{1,0:T(8,128)} fusion(bf16[1536,2048]{1,0:T(8,128)(2,1)} %get-tuple-element.94.refs_5_.refs_0_, bf16[1536,1024]{1,0:T(8,128)(2,1)} %get-tuple-element.108), kind=kOutput, calls=%fused_computation.49 | convolution fusion | flops 6442450944 | bytes 17825792 | tf_op jit(solution)/shard_map/dot_general | solution.py:493
  495.5 13.2 %collective-permute-done.51.refs_4_ = bf16[2,128,2048]{2,1,0:T(8,128)(2,1)} collective-permute-done((bf16[2,128,2048]{2,1,0:T(8,128)(2,1)}, bf16[2,128,2048]{2,1,0:T(8,128)(2,1)}, u32[]{:S(2)}, u32[]{:S(2)}) %collective-permute-start.51) | collective-permute-done | bytes 1048608 | tf_op jit(solution)/shard_map/ppermute | solution.py:438
  526.5 8.9 %fusion = bf16[1024,1,2048]{2,0,1:T(8,128)(2,1)} fusion(f32[1024,2048]{1,0:T(8,128)} %fusion.22.refs_6_, bf16[512,2048]{1,0:T(8,128)(2,1)} %get-tuple-element.103.refs_0_, bf16[256,1024]{1,0:T(8,128)(2,1)} %get-tuple-element.107, bf16[256,1024]{1,0:T(8,128)(2,1)} %get-tuple-element.105), kind=kOutput, calls=%fused_computation.2 | convolution fusion | flops 2153775104 | bytes 15728640 | tf_op jit(solution)/shard_map/dot_general | solution.py:493
  535.4 7.9 %fusion.1 = bf16[1,2048,1024]{2,1,0:T(8,128)(2,1)} fusion(f32[2048,1024]{1,0:T(8,128)} %fusion.23.refs_4_, bf16[512,2048]{1,0:T(8,128)(2,1)S(1)} %copy-done, bf16[256,1024]{1,0:T(8,128)(2,1)S(1)} %copy-done.4, bf16[256,1024]{1,0:T(8,128)(2,1)S(1)} %copy-done.5), kind=kOutput, calls=%fused_computation.3 | convolution fusion | flops 2153775104 | bytes 15728640 | tf_op jit(solution)/shard_map/dot_general | solution.py:493
  (203 shorter events, 360.9 us)
Async XLA Ops:
  14.0 26.7 %collective-permute-start.2 = (bf16[2,256,1024]{2,1,0:T(8,128)(2,1)}, bf16[2,256,1024]{2,1,0:T(8,128)(2,1)}, u32[]{:S(2)}, u32[]{:S(2)}) collective-permute-start(bf16[2,256,1024]{2,1,0:T(8,128)(2,1)} %pack.4.refs_2_), channel_id=1, source_target_pairs={{0,1},{1,0},{2,3},{3,2},{4,5},{5,4},{6,7},{7,6},{8,9},{9,8},{10,11... | collective-permute-start | bytes 3145736 | tf_op jit(solution)/shard_map/ppermute | solution.py:400
  17.6 24.8 %collective-permute-start.4 = (bf16[2,128,2048]{2,1,0:T(8,128)(2,1)}, bf16[2,128,2048]{2,1,0:T(8,128)(2,1)}, u32[]{:S(2)}, u32[]{:S(2)}) collective-permute-start(bf16[2,128,2048]{2,1,0:T(8,128)(2,1)} %pack.5.refs_4_), channel_id=1, source_target_pairs={{16,20},{20,24},{24,28},{4,0},{8,4},{12,8},{28,12},{0,16},{17,21},... | collective-permute-start | bytes 3145736 | tf_op jit(solution)/shard_map/ppermute | solution.py:438
  40.8 25.9 %collective-permute-start.6 = (bf16[2,256,1024]{2,1,0:T(8,128)(2,1)}, bf16[2,256,1024]{2,1,0:T(8,128)(2,1)}, u32[]{:S(2)}, u32[]{:S(2)}) collective-permute-start(bf16[2,256,1024]{2,1,0:T(8,128)(2,1)} %pack.4.refs_2_), channel_id=1, source_target_pairs={{0,2},{1,3},{2,0},{3,1},{4,6},{5,7},{6,4},{7,5},{8,10},{9,11},{10,... | collective-permute-start | bytes 3145736 | tf_op jit(solution)/shard_map/ppermute | solution.py:400
  44.9 24.3 %collective-permute-start.8 = (bf16[2,128,2048]{2,1,0:T(8,128)(2,1)}, bf16[2,128,2048]{2,1,0:T(8,128)(2,1)}, u32[]{:S(2)}, u32[]{:S(2)}) collective-permute-start(bf16[2,128,2048]{2,1,0:T(8,128)(2,1)} %chain_step.35.refs_4_), channel_id=1, source_target_pairs={{16,20},{20,24},{24,28},{4,0},{8,4},{12,8},{28,12},{0,16},{17,21},... | collective-permute-start | bytes 3145736 | tf_op jit(solution)/shard_map/ppermute | solution.py:438
  54.2 24.3 %collective-permute-start.5 = (bf16[2,128,2048]{2,1,0:T(8,128)(2,1)}, bf16[2,128,2048]{2,1,0:T(8,128)(2,1)}, u32[]{:S(2)}, u32[]{:S(2)}) collective-permute-start(bf16[2,128,2048]{2,1,0:T(8,128)(2,1)} %chain_step.36.refs_4_), channel_id=1, source_target_pairs={{0,4},{4,8},{8,12},{20,16},{24,20},{28,24},{12,28},{16,0},{1,5},{5... | collective-permute-start | bytes 3145736 | tf_op jit(solution)/shard_map/ppermute | solution.py:438
  66.7 26.6 %collective-permute-start.11 = (bf16[2,256,1024]{2,1,0:T(8,128)(2,1)}, bf16[2,256,1024]{2,1,0:T(8,128)(2,1)}, u32[]{:S(2)}, u32[]{:S(2)}) collective-permute-start(bf16[2,256,1024]{2,1,0:T(8,128)(2,1)} %hold.4.refs_7_.refs_1_.refs_3_), channel_id=1, source_target_pairs={{0,1},{1,0},{2,3},{3,2},{4,5},{5,4},{6,7},{7,6},{8,9},{9,8},{10,11... | collective-permute-start | bytes 3145736 | tf_op jit(solution)/shard_map/ppermute | solution.py:400
  123.7 26.7 %collective-permute-start.17 = (bf16[2,128,2048]{2,1,0:T(8,128)(2,1)}, bf16[2,128,2048]{2,1,0:T(8,128)(2,1)}, u32[]{:S(2)}, u32[]{:S(2)}) collective-permute-start(bf16[2,128,2048]{2,1,0:T(8,128)(2,1)} %chain_step.42.refs_10_), channel_id=1, source_target_pairs={{0,4},{4,8},{8,12},{20,16},{24,20},{28,24},{12,28},{16,0},{1,5},{5... | collective-permute-start | bytes 3145736 | tf_op jit(solution)/shard_map/ppermute | solution.py:438
  192.0 24.0 %collective-permute-start.22 = (bf16[2,128,2048]{2,1,0:T(8,128)(2,1)}, bf16[2,128,2048]{2,1,0:T(8,128)(2,1)}, u32[]{:S(2)}, u32[]{:S(2)}) collective-permute-start(bf16[2,128,2048]{2,1,0:T(8,128)(2,1)} %chain_step.47.refs_2_), channel_id=1, source_target_pairs={{16,20},{20,24},{24,28},{4,0},{8,4},{12,8},{28,12},{0,16},{17,21},... | collective-permute-start | bytes 3145736 | tf_op jit(solution)/shard_map/ppermute | solution.py:438
  199.7 26.0 %collective-permute-start.23 = (bf16[2,128,2048]{2,1,0:T(8,128)(2,1)}, bf16[2,128,2048]{2,1,0:T(8,128)(2,1)}, u32[]{:S(2)}, u32[]{:S(2)}) collective-permute-start(bf16[2,128,2048]{2,1,0:T(8,128)(2,1)} %chain_step.48.refs_10_), channel_id=1, source_target_pairs={{0,4},{4,8},{8,12},{20,16},{24,20},{28,24},{12,28},{16,0},{1,5},{5... | collective-permute-start | bytes 3145736 | tf_op jit(solution)/shard_map/ppermute | solution.py:438
  228.2 25.6 %collective-permute-start.27 = (bf16[2,128,2048]{2,1,0:T(8,128)(2,1)}, bf16[2,128,2048]{2,1,0:T(8,128)(2,1)}, u32[]{:S(2)}, u32[]{:S(2)}) collective-permute-start(bf16[2,128,2048]{2,1,0:T(8,128)(2,1)} %chain_step.50.refs_10_), channel_id=1, source_target_pairs={{0,4},{4,8},{8,12},{20,16},{24,20},{28,24},{12,28},{16,0},{1,5},{5... | collective-permute-start | bytes 3145736 | tf_op jit(solution)/shard_map/ppermute | solution.py:438
  256.3 25.7 %collective-permute-start.29 = (bf16[2,128,2048]{2,1,0:T(8,128)(2,1)}, bf16[2,128,2048]{2,1,0:T(8,128)(2,1)}, u32[]{:S(2)}, u32[]{:S(2)}) collective-permute-start(bf16[2,128,2048]{2,1,0:T(8,128)(2,1)} %chain_step.52.refs_10_), channel_id=1, source_target_pairs={{0,4},{4,8},{8,12},{20,16},{24,20},{28,24},{12,28},{16,0},{1,5},{5... | collective-permute-start | bytes 3145736 | tf_op jit(solution)/shard_map/ppermute | solution.py:438
  266.2 26.6 %collective-permute-start.30 = (bf16[2,128,2048]{2,1,0:T(8,128)(2,1)}, bf16[2,128,2048]{2,1,0:T(8,128)(2,1)}, u32[]{:S(2)}, u32[]{:S(2)}) collective-permute-start(bf16[2,128,2048]{2,1,0:T(8,128)(2,1)} %chain_step.53.refs_2_), channel_id=1, source_target_pairs={{16,20},{20,24},{24,28},{4,0},{8,4},{12,8},{28,12},{0,16},{17,21},... | collective-permute-start | bytes 3145736 | tf_op jit(solution)/shard_map/ppermute | solution.py:438
  284.5 27.7 %collective-permute-start.32 = (bf16[2,128,2048]{2,1,0:T(8,128)(2,1)}, bf16[2,128,2048]{2,1,0:T(8,128)(2,1)}, u32[]{:S(2)}, u32[]{:S(2)}) collective-permute-start(bf16[2,128,2048]{2,1,0:T(8,128)(2,1)} %chain_step.54.refs_10_), channel_id=1, source_target_pairs={{0,4},{4,8},{8,12},{20,16},{24,20},{28,24},{12,28},{16,0},{1,5},{5... | collective-permute-start | bytes 3145736 | tf_op jit(solution)/shard_map/ppermute | solution.py:438
  295.3 25.5 %collective-permute-start.33 = (bf16[2,128,2048]{2,1,0:T(8,128)(2,1)}, bf16[2,128,2048]{2,1,0:T(8,128)(2,1)}, u32[]{:S(2)}, u32[]{:S(2)}) collective-permute-start(bf16[2,128,2048]{2,1,0:T(8,128)(2,1)} %chain_step.55.refs_2_), channel_id=1, source_target_pairs={{16,20},{20,24},{24,28},{4,0},{8,4},{12,8},{28,12},{0,16},{17,21},... | collective-permute-start | bytes 3145736 | tf_op jit(solution)/shard_map/ppermute | solution.py:438
  314.6 26.1 %collective-permute-start.34 = (bf16[2,128,2048]{2,1,0:T(8,128)(2,1)}, bf16[2,128,2048]{2,1,0:T(8,128)(2,1)}, u32[]{:S(2)}, u32[]{:S(2)}) collective-permute-start(bf16[2,128,2048]{2,1,0:T(8,128)(2,1)} %chain_step.56.refs_10_), channel_id=1, source_target_pairs={{0,4},{4,8},{8,12},{20,16},{24,20},{28,24},{12,28},{16,0},{1,5},{5... | collective-permute-start | bytes 3145736 | tf_op jit(solution)/shard_map/ppermute | solution.py:438
  323.4 24.6 %collective-permute-start.36 = (bf16[2,128,2048]{2,1,0:T(8,128)(2,1)}, bf16[2,128,2048]{2,1,0:T(8,128)(2,1)}, u32[]{:S(2)}, u32[]{:S(2)}) collective-permute-start(bf16[2,128,2048]{2,1,0:T(8,128)(2,1)} %chain_step.57.refs_2_), channel_id=1, source_target_pairs={{16,20},{20,24},{24,28},{4,0},{8,4},{12,8},{28,12},{0,16},{17,21},... | collective-permute-start | bytes 3145736 | tf_op jit(solution)/shard_map/ppermute | solution.py:438
  363.4 30.0 %collective-permute-start.41 = (bf16[2,128,2048]{2,1,0:T(8,128)(2,1)}, bf16[2,128,2048]{2,1,0:T(8,128)(2,1)}, u32[]{:S(2)}, u32[]{:S(2)}) collective-permute-start(bf16[2,128,2048]{2,1,0:T(8,128)(2,1)} %chain_step.60.refs_10_), channel_id=1, source_target_pairs={{0,4},{4,8},{8,12},{20,16},{24,20},{28,24},{12,28},{16,0},{1,5},{5... | collective-permute-start | bytes 3145736 | tf_op jit(solution)/shard_map/ppermute | solution.py:438
  395.9 29.5 %collective-permute-start.44 = (bf16[2,128,2048]{2,1,0:T(8,128)(2,1)}, bf16[2,128,2048]{2,1,0:T(8,128)(2,1)}, u32[]{:S(2)}, u32[]{:S(2)}) collective-permute-start(bf16[2,128,2048]{2,1,0:T(8,128)(2,1)} %chain_step.62.refs_10_), channel_id=1, source_target_pairs={{0,4},{4,8},{8,12},{20,16},{24,20},{28,24},{12,28},{16,0},{1,5},{5... | collective-permute-start | bytes 3145736 | tf_op jit(solution)/shard_map/ppermute | solution.py:438
  401.9 48.0 %collective-permute-start.48 = (bf16[256,1024]{1,0:T(8,128)(2,1)}, bf16[256,1024]{1,0:T(8,128)(2,1)}, u32[]{:S(2)}, u32[]{:S(2)}) collective-permute-start(bf16[256,1024]{1,0:T(8,128)(2,1)} %add_convert_fusion.6.refs_4_), channel_id=1, source_target_pairs={{0,2},{1,3},{2,0},{3,1},{4,6},{5,7},{6,4},{7,5},{8,10},{9,11},{10,... | collective-permute-start | bytes 1572872 | tf_op jit(solution)/shard_map/ppermute | solution.py:400
  408.4 26.9 %collective-permute-start.46 = (bf16[2,128,2048]{2,1,0:T(8,128)(2,1)}, bf16[2,128,2048]{2,1,0:T(8,128)(2,1)}, u32[]{:S(2)}, u32[]{:S(2)}) collective-permute-start(bf16[2,128,2048]{2,1,0:T(8,128)(2,1)} %chain_step.63.refs_2_), channel_id=1, source_target_pairs={{16,20},{20,24},{24,28},{4,0},{8,4},{12,8},{28,12},{0,16},{17,21},... | collective-permute-start | bytes 3145736 | tf_op jit(solution)/shard_map/ppermute | solution.py:438
  427.9 27.2 %collective-permute-start.45 = (bf16[2,128,2048]{2,1,0:T(8,128)(2,1)}, bf16[2,128,2048]{2,1,0:T(8,128)(2,1)}, u32[]{:S(2)}, u32[]{:S(2)}) collective-permute-start(bf16[2,128,2048]{2,1,0:T(8,128)(2,1)} %chain_step.64.refs_8_), channel_id=1, source_target_pairs={{0,4},{4,8},{8,12},{20,16},{24,20},{28,24},{12,28},{16,0},{1,5},{5... | collective-permute-start | bytes 3145736 | tf_op jit(solution)/shard_map/ppermute | solution.py:438
  483.7 25.1 %collective-permute-start.51 = (bf16[2,128,2048]{2,1,0:T(8,128)(2,1)}, bf16[2,128,2048]{2,1,0:T(8,128)(2,1)}, u32[]{:S(2)}, u32[]{:S(2)}) collective-permute-start(bf16[2,128,2048]{2,1,0:T(8,128)(2,1)} %chain_step.66.refs_10_), channel_id=1, source_target_pairs={{0,4},{4,8},{8,12},{20,16},{24,20},{28,24},{12,28},{16,0},{1,5},{5... | collective-permute-start | bytes 3145736 | tf_op jit(solution)/shard_map/ppermute | solution.py:438
  485.7 23.8 %collective-permute-start.52 = (bf16[2,128,2048]{2,1,0:T(8,128)(2,1)}, bf16[2,128,2048]{2,1,0:T(8,128)(2,1)}, u32[]{:S(2)}, u32[]{:S(2)}) collective-permute-start(bf16[2,128,2048]{2,1,0:T(8,128)(2,1)} %chain_step.67.refs_10_), channel_id=1, source_target_pairs={{16,20},{20,24},{24,28},{4,0},{8,4},{12,8},{28,12},{0,16},{17,21},... | collective-permute-start | bytes 3145736 | tf_op jit(solution)/shard_map/ppermute | solution.py:438
  520.6 25.4 %collective-permute-start.55 = (f32[256,1024]{1,0:T(8,128)}, f32[256,1024]{1,0:T(8,128)}, u32[]{:S(2)}, u32[]{:S(2)}) collective-permute-start(f32[256,1024]{1,0:T(8,128)} %share_of.30.refs_2_), channel_id=1, source_target_pairs={{0,16},{16,0},{1,17},{17,1},{2,18},{18,2},{3,19},{19,3},{4,20},{20... | collective-permute-start | bytes 3145736 | tf_op jit(solution)/shard_map/ppermute | solution.py:397
  (39 other events, 636.2 us)

commit v2 on v1

v2 whole, which is shorter than its diff:
```python
import functools
import math

import jax
import jax.numpy as jnp
from jax import lax
from jax.experimental import pallas as pl
from jax.experimental.pallas import tpu as pltpu
from jax.sharding import PartitionSpec as P

ROWS = 128
VMEM_MIB = 64
REST_AT = (2, 0)
PROJECT_AT = ((1, 1), (2, 1), (4, 0), (5, 0), (7, 0), (9, 0), (11, 0))
PROJECT_COLS = 1024
PARTIAL = jnp.float32
ANY = pl.BlockSpec(memory_space=pltpu.HBM)
SMALL = pl.CostEstimate(flops=1024, bytes_accessed=1024, transcendentals=0)


def params(mib):
    return pltpu.CompilerParams(vmem_limit_bytes=mib << 20)


def hbm_out(shape, dtype=jnp.bfloat16):
    return jax.ShapeDtypeStruct(shape, dtype)


def row_chunks(rows, hidden):
    parts = 2 if rows % 32 == 0 and rows * hidden >= 1 << 17 else 1
    return [(i * (rows // parts), rows // parts) for i in range(parts)]


def across(left, right):
    return lax.dot_general(left, right, (((1,), (1,)), ((), ())), preferred_element_type=jnp.float32)


def project(streams, blocks, weights, replica, hidden, as_sent, after):
    width = blocks[0][0][0].shape[1]
    tile = min(PROJECT_COLS, hidden)
    steps = hidden // tile
    operands, specs, out_specs, out_shape = [], [], [], []
    types = [PARTIAL, jnp.bfloat16] if as_sent else [PARTIAL]
    for s in streams:
        operands.append(weights[s])
        if s == 0:
            specs.append(pl.BlockSpec((width, tile), lambda i, d: (0, d[0] * steps + i)))
        else:
            specs.append(pl.BlockSpec((tile, width), lambda i, d: (d[0] * steps + i, 0)))
        for pair, first, rows in blocks:
            at = first // rows
            if isinstance(pair, tuple):
                operands.append(pair[s])
                specs.append(pl.BlockSpec((rows, width), lambda i, d, at=at: (at, 0)))
            else:
                operands.append(pair)
                specs.append(pl.BlockSpec((None, rows, width), lambda i, d, s=s, at=at: (s, at, 0)))
            for out_type in types:
                out_specs.append(pl.BlockSpec((rows, tile), lambda i, d: (0, i)))
                out_shape.append(hbm_out((rows, hidden), out_type))

    def body(replica_ref, *refs):
        outs = iter(refs[len(operands) + len(after) :])
        given = iter(refs)
        for s in streams:
            weight = next(given)[...]
            for _ in blocks:
                x = next(given)[...]
                if s == 0:
                    value = jnp.dot(x, weight, preferred_element_type=jnp.float32)
                else:
                    value = across(x, weight)
                for _ in types:
                    out = next(outs)
                    out[...] = value.astype(out.dtype)

    return pl.pallas_call(
        body,
        grid_spec=pltpu.PrefetchScalarGridSpec(
            num_scalar_prefetch=1,
            grid=(steps,),
            in_specs=specs + [ANY] * len(after),
            out_specs=out_specs,
        ),
        out_shape=out_shape,
        compiler_params=params(VMEM_MIB),
        cost_estimate=SMALL,
        name="project",
    )(replica, *operands, *after)


def pack(pair, after):
    def body(*refs):
        out, held, in_sem, out_sem = refs[-4:]
        into = [pltpu.make_async_copy(refs[i], held.at[i], in_sem.at[i]) for i in range(2)]
        out_of = [pltpu.make_async_copy(held.at[i], out.at[i], out_sem.at[i]) for i in range(2)]
        for copy in into:
            copy.start()
        for i in range(2):
            into[i].wait()
            out_of[i].start()
        for copy in out_of:
            copy.wait()

    shape = (2, *pair[0].shape)
    return pl.pallas_call(
        body,
        in_specs=[ANY] * (2 + len(after)),
        out_specs=ANY,
        out_shape=hbm_out(shape),
        scratch_shapes=[
            pltpu.VMEM(shape, pair[0].dtype),
            pltpu.SemaphoreType.DMA((2,)),
            pltpu.SemaphoreType.DMA((2,)),
        ],
        compiler_params=params(VMEM_MIB),
        cost_estimate=SMALL,
        name="pack",
    )(*pair, *after)


def total_of(terms, after):
    rows, cols = terms[0][0].shape
    n = len(terms[0])

    def body(*refs):
        outs = refs[2 * n + len(after) :]
        for s in range(2):
            value = refs[s * n][...].astype(jnp.float32)
            for i in range(1, n):
                value = value + refs[s * n + i][...].astype(jnp.float32)
            outs[s][...] = value.astype(jnp.bfloat16)

    steps = 4 if rows % 64 == 0 else 1
    spec = pl.BlockSpec((rows // steps, cols), lambda i: (i, 0))
    return pl.pallas_call(
        body,
        grid=(steps,),
        in_specs=[spec] * (2 * n) + [ANY] * len(after),
        out_specs=[spec] * 2,
        out_shape=[hbm_out((rows, cols))] * 2,
        compiler_params=params(VMEM_MIB),
        cost_estimate=SMALL,
        name="total_of",
    )(*terms[0], *terms[1], *after)


def hold(array, after):
    return pl.pallas_call(
        lambda *refs: None,
        in_specs=[ANY] * (1 + len(after)),
        out_specs=ANY,
        out_shape=hbm_out(array.shape, array.dtype),
        input_output_aliases={0: 0},
        compiler_params=params(VMEM_MIB),
        cost_estimate=SMALL,
        name="hold",
    )(array, *after)


def own_place(ring, line):
    row = lax.axis_index("row")
    return jnp.where(lax.axis_index("dp") == ring, row, line - 1 - row)


def apart(after, arrays):
    return [a for a in after if all(a is not b for b in arrays)]


def distinct(arrays):
    found = []
    for array in arrays:
        if all(array is not seen for seen in found):
            found.append(array)
    return found, [next(i for i, seen in enumerate(found) if seen is a) for a in arrays]


def chain_step(got, partials, after):
    rows, hidden = got[0].shape
    late = len(partials)
    chunks = row_chunks(rows, hidden)
    arrays, which = distinct([array for array, _ in partials])

    def body(*refs):
        got_h, terms = refs[:2], refs[2 : 2 + len(arrays)]
        out_h = refs[2 + len(arrays) + len(after) :][:2]
        got_v, own_v, out_v, got_sem, own_sem, out_sem = refs[-6:]
        places = [own_place(ring, late) for ring in range(2)]

        def own_copy(j, ring, c):
            first, count = chunks[c]
            return pltpu.make_async_copy(
                terms[which[j]].at[pl.ds(partials[j][1] + first, count)],
                own_v.at[ring, pl.ds(first, count)],
                own_sem.at[ring, c],
            )

        for ring in range(2):
            for j in range(late):

                @pl.when(places[ring] == j)
                def _(ring=ring, j=j):
                    for c in range(len(chunks)):
                        own_copy(j, ring, c).start()

        copies = []
        for c, (first, count) in enumerate(chunks):
            part = pl.ds(first, count)
            for ring in range(2):
                got_copy = pltpu.make_async_copy(
                    got_h[ring].at[part], got_v.at[ring, part], got_sem.at[ring, c]
                )
                out_copy = pltpu.make_async_copy(
                    out_v.at[ring, part], out_h[ring].at[part], out_sem.at[ring, c]
                )
                got_copy.start()
                copies.append((ring, part, got_copy, own_copy(0, ring, c), out_copy))
        for ring, part, got_copy, mine, out_copy in copies:
            got_copy.wait()
            mine.wait()
            before = jnp.where(places[ring] == 0, 0.0, got_v[ring, part].astype(jnp.float32))
            out_v[ring, part] = (before + own_v[ring, part]).astype(out_v.dtype)
            out_copy.start()
        for copy in copies:
            copy[-1].wait()

    return pl.pallas_call(
        body,
        in_specs=[ANY] * (2 + len(arrays) + len(after)),
        out_specs=[ANY] * 2,
        out_shape=[hbm_out((rows, hidden))] * 2,
        scratch_shapes=[
            pltpu.VMEM((2, rows, hidden), jnp.bfloat16),
            pltpu.VMEM((2, rows, hidden), PARTIAL),
            pltpu.VMEM((2, rows, hidden), jnp.bfloat16),
        ]
        + [pltpu.SemaphoreType.DMA((2, len(chunks)))] * 3,
        compiler_params=params(VMEM_MIB),
        cost_estimate=SMALL,
        name="chain_step",
    )(*got, *arrays, *after)


def activate(partial, got, kept, kept_rows, kept_row, after):
    rows, hidden = got[0][0][0].shape
    line = len(got[0][0]) + 1
    after = apart(after, kept)
    given, which = distinct([*partial[:2], *(a for ring in got for stream in ring for a in stream)])
    step_rows, step_cols = 16, min(512, hidden)
    halves = len(row_chunks(rows, hidden))
    part_rows = rows // halves
    across_cols = hidden // step_cols
    tiles = (part_rows // step_rows) * across_cols

    def body(*refs):
        terms = refs[: len(given)]
        outs = refs[len(given) + len(kept) + len(after) :][:2]
        own_v, got_v, out_v, own_sem, got_sem, out_sem = refs[-6:]

        def own_copy(s, h):
            part = pl.ds(h * part_rows, part_rows)
            return pltpu.make_async_copy(
                terms[which[s]].at[pl.ds(partial[2] + h * part_rows, part_rows)],
                own_v.at[s, part],
                own_sem.at[s, h],
            )

        def got_copy(ring, j, s, h):
            part = pl.ds(h * part_rows, part_rows)
            return pltpu.make_async_copy(
                terms[which[2 + (2 * ring + s) * (line - 1) + j]].at[part],
                got_v.at[ring, s, part],
                got_sem.at[ring, s, h],
            )

        for h in range(halves):
            for s in range(2):
                own_copy(s, h).start()
                for ring in range(2):
                    place = own_place(ring, line)

                    @pl.when(place == 0)
                    def _(ring=ring, s=s, h=h):
                        part = pl.ds(h * part_rows, part_rows)
                        got_v[ring, s, part] = jnp.zeros((part_rows, hidden), got_v.dtype)

                    for j in range(1, line):

                        @pl.when(place == j)
                        def _(ring=ring, j=j, s=s, h=h):
                            got_copy(ring, j - 1, s, h).start()

        out_copies = []
        for h in range(halves):
            for s in range(2):
                own_copy(s, h).wait()
                for ring in range(2):

                    @pl.when(own_place(ring, line) != 0)
                    def _(ring=ring, s=s, h=h):
                        got_copy(ring, 0, s, h).wait()

            def tile(i, _, h=h):
                at = pl.multiple_of((i // across_cols) * step_rows, step_rows)
                r = pl.ds(h * part_rows + at, step_rows)
                c = pl.ds(pl.multiple_of((i % across_cols) * step_cols, step_cols), step_cols)
                pre, grad = (
                    own_v[s, r, c].astype(jnp.float32)
                    + got_v[0, s, r, c].astype(jnp.float32)
                    + got_v[1, s, r, c].astype(jnp.float32)
                    for s in range(2)
                )
                cdf = 0.5 * (1.0 + lax.erf(pre * (1.0 / math.sqrt(2.0))))
                pdf = jnp.exp(-0.5 * pre * pre) * (1.0 / math.sqrt(2.0 * math.pi))
                out_v[0, r, c] = (pre * cdf).astype(jnp.bfloat16)
                out_v[1, r, c] = (grad * (cdf + pre * pdf)).astype(jnp.bfloat16)
                return 0

            lax.fori_loop(0, tiles, tile, 0)
            for i in range(2):
                copy = pltpu.make_async_copy(
                    out_v.at[i, pl.ds(h * part_rows, part_rows)],
                    outs[i].at[pl.ds(kept_row + h * part_rows, part_rows)],
                    out_sem.at[i, h],
                )
                copy.start()
                out_copies.append(copy)
        for copy in out_copies:
            copy.wait()

    return pl.pallas_call(
        body,
        in_specs=[ANY] * (len(given) + len(kept) + len(after)),
        out_specs=[ANY] * 2,
        out_shape=[hbm_out((kept_rows, hidden))] * 2,
        input_output_aliases={len(given) + i: i for i in range(len(kept))},
        scratch_shapes=[
            pltpu.VMEM((2, rows, hidden), PARTIAL),
            pltpu.VMEM((2, 2, rows, hidden), jnp.bfloat16),
            pltpu.VMEM((2, rows, hidden), jnp.bfloat16),
            pltpu.SemaphoreType.DMA((2, halves)),
            pltpu.SemaphoreType.DMA((2, 2, halves)),
            pltpu.SemaphoreType.DMA((2, halves)),
        ],
        compiler_params=params(VMEM_MIB),
        cost_estimate=SMALL,
        name="activate",
    )(*given, *kept, *after)


def share_of(hid, first, rows, weights, out_type, after):
    hidden = hid[0].shape[1]
    width = weights[0].shape[1]

    def body(*refs):
        hid_h, weight_h = refs[:2], refs[2:4]
        out_h = refs[4 + len(after) :][:2]
        hid_v, w_out_v, w_in_v, out_v, hid_sem, weight_sem, out_sem = refs[-7:]
        mine = pl.ds(pl.multiple_of(lax.axis_index("dp") * hidden, hidden), hidden)
        part = pl.ds(first, rows)
        hid_copies = [
            pltpu.make_async_copy(hid_h[i].at[part], hid_v.at[i], hid_sem.at[i]) for i in range(2)
        ]
        weight_copies = [
            pltpu.make_async_copy(weight_h[0].at[mine], w_out_v, weight_sem.at[0]),
            pltpu.make_async_copy(weight_h[1].at[:, mine], w_in_v, weight_sem.at[1]),
        ]
        out_copies = [
            pltpu.make_async_copy(out_v.at[i], out_h[i], out_sem.at[i]) for i in range(2)
        ]
        for i in range(2):
            hid_copies[i].start()
            weight_copies[i].start()
        for i in range(2):
            hid_copies[i].wait()
            weight_copies[i].wait()
            if i == 0:
                value = jnp.dot(hid_v[0], w_out_v[...], preferred_element_type=jnp.float32)
            else:
                value = across(hid_v[1], w_in_v[...])
            out_v[i] = value.astype(out_type)
            out_copies[i].start()
        for copy in out_copies:
            copy.wait()

    return pl.pallas_call(
        body,
        in_specs=[ANY] * (4 + len(after)),
        out_specs=[ANY] * 2,
        out_shape=[hbm_out((rows, width), out_type)] * 2,
        scratch_shapes=[
            pltpu.VMEM((2, rows, hidden), jnp.bfloat16),
            pltpu.VMEM((hidden, width), jnp.bfloat16),
            pltpu.VMEM((width, hidden), jnp.bfloat16),
            pltpu.VMEM((2, rows, width), out_type),
            pltpu.SemaphoreType.DMA((2,)),
            pltpu.SemaphoreType.DMA((2,)),
            pltpu.SemaphoreType.DMA((2,)),
        ],
        compiler_params=params(VMEM_MIB),
        cost_estimate=SMALL,
        name="share_of",
    )(*hid, *weights, *after)


def add_pair(left, right, after):
    rows, cols = left.shape

    def body(left_ref, right_ref, *rest):
        rest[-1][...] = (left_ref[...] + right_ref[...].astype(jnp.float32)).astype(jnp.bfloat16)

    steps = 2 if rows % 32 == 0 else 1
    spec = pl.BlockSpec((rows // steps, cols), lambda i: (i, 0))
    return pl.pallas_call(
        body,
        grid=(steps,),
        in_specs=[spec, spec] + [ANY] * len(after),
        out_specs=spec,
        out_shape=hbm_out((rows, cols)),
        compiler_params=params(VMEM_MIB),
        cost_estimate=SMALL,
        name="add_pair",
    )(left, right, *after)


def gradients(blocks, hid, after):
    _, block, width = blocks[0].shape
    depth, hidden = hid[0].shape
    n = len(blocks)
    given = [*blocks, *hid]
    sizes = [(width, hidden), (hidden, width)]
    tall = min(512, width, hidden)

    def body(*refs):
        act_h, grad_h = refs[n : n + 2]
        out_h = refs[len(given) + len(after) :][:2]
        x_v, grad_v, act_v, g_v, in_v, out_v, block_sem, hid_sem, in_sem, out_sem = refs[-10:]
        sides = [(x_v, grad_h, grad_v), (g_v, act_h, act_v)]
        copies = [[], []]
        for which, (blocks_v, hid_h, hid_v) in enumerate(sides):
            for i in range(n):
                rows = pl.ds(i * block, block)
                copies[which] += [
                    pltpu.make_async_copy(
                        refs[i].at[which], blocks_v.at[rows], block_sem.at[which, i]
                    ),
                    pltpu.make_async_copy(hid_h.at[rows], hid_v.at[rows], hid_sem.at[which, i]),
                ]
            for copy in copies[which]:
                copy.start()
        done = []
        for which, (left, right, result_v, sem) in enumerate(
            [(x_v, grad_v, in_v, in_sem), (act_v, g_v, out_v, out_sem)]
        ):
            for copy in copies[which]:
                copy.wait()

            def part(i, _, left=left, right=right, result_v=result_v, sem=sem, which=which):
                rows = pl.ds(pl.multiple_of(i * tall, tall), tall)
                result_v[rows] = lax.dot_general(
                    left[:, rows],
                    right[...],
                    (((0,), (0,)), ((), ())),
                    preferred_element_type=jnp.float32,
                ).astype(jnp.bfloat16)
                pltpu.make_async_copy(result_v.at[rows], out_h[which].at[rows], sem.at[i]).start()
                return 0

            lax.fori_loop(0, sizes[which][0] // tall, part, 0)
            for i in range(sizes[which][0] // tall):
                rows = pl.ds(i * tall, tall)
                done.append(
                    pltpu.make_async_copy(result_v.at[rows], out_h[which].at[rows], sem.at[i])
                )
        for copy in done:
            copy.wait()

    return pl.pallas_call(
        body,
        in_specs=[ANY] * (len(given) + len(after)),
        out_specs=[ANY] * 2,
        out_shape=[hbm_out(size) for size in sizes],
        scratch_shapes=[
            pltpu.VMEM((depth, width), jnp.bfloat16),
            pltpu.VMEM((depth, hidden), jnp.bfloat16),
            pltpu.VMEM((depth, hidden), jnp.bfloat16),
            pltpu.VMEM((depth, width), jnp.bfloat16),
            pltpu.VMEM(sizes[0], jnp.bfloat16),
            pltpu.VMEM(sizes[1], jnp.bfloat16),
            pltpu.SemaphoreType.DMA((2, n)),
            pltpu.SemaphoreType.DMA((2, n)),
            pltpu.SemaphoreType.DMA((width // tall,)),
            pltpu.SemaphoreType.DMA((hidden // tall,)),
        ],
        compiler_params=params(VMEM_MIB),
        cost_estimate=SMALL,
        name="gradients",
    )(*given, *after)


def on_device(line, cols, tokens, w_in, w_out, out_grad):
    block, width = tokens.shape
    hidden = w_in.shape[1] // 2
    rows = min(ROWS, block)
    per = block // rows
    replica = lax.axis_index("dp").astype(jnp.int32).reshape(1)

    def ring_pairs(ring):
        up, down = ring * line, (1 - ring) * line
        pairs = [(up + i, up + i + 1) for i in range(line - 1)]
        pairs += [(down + i + 1, down + i) for i in range(line - 1)]
        return [*pairs, (up + line - 1, down + line - 1), (down, up)]

    def over_dp(x):
        return lax.ppermute(x, "dp", [(0, 1), (1, 0)])

    def over_col(x, k):
        return lax.ppermute(x, "col", [(i, i ^ k) for i in range(cols)])

    order = [(0, 0)] + [(d, k) for k in range(1, cols) for d in range(2)] + [(1, 0)]
    final = len(order) - 1
    count = len(order) * per
    last = []
    own = (tokens, out_grad)
    xg = {(0, 0): own}
    first = {}
    partial = {}
    came = [[[], []], [[], []]]
    kept = ()
    shares = {}
    swapped = {}
    pairs = {}
    collected = {}

    def project_blocks(streams, parts, as_sent=False):
        nonlocal last
        blocks = [part[1:] for part in parts]
        done = project(streams, blocks, (w_in, w_out), replica, hidden, as_sent, last)
        arrays = iter(done)
        for s in streams:
            for b, _, _, n in parts:
                array = next(arrays)
                for i in range(n // rows):
                    partial.setdefault(b + i, [None, None, i * rows])[s] = array
                if as_sent:
                    first[s] = next(arrays)
        last = [done[-1]]

    def project_one(r):
        project_blocks((0, 1), [(r * per, xg[order[r]], 0, block)])

    def step(stream, t):
        nonlocal last
        if t == 0:
            send = [first[stream]] * 2
        else:
            terms = [partial[min(max(t - j, 0), count - 1)] for j in range(line)]
            got = [came[ring][stream][t - 1] for ring in range(2)]
            send = chain_step(got, [(term[stream], term[2]) for term in terms], last)
        last = [send[0]]
        for ring in range(2):
            came[ring][stream].append(lax.ppermute(send[ring], ("dp", "row"), ring_pairs(ring)))

    def gather_own():
        nonlocal last
        xg[0, 0] = pack(own, last)
        last = [xg[0, 0]]
        spread_from(1, cols if not staged else 2)

    def spread_from(first_k, end):
        for k in range(first_k, end):
            low = k & -k
            xg[0, k] = over_col(xg[0, k ^ low], low)
        for k in range(first_k, end):
            xg[1, k] = over_dp(xg[0, k])
        if end == cols:
            xg[1, 0] = over_dp(xg[0, 0])

    def gather_rest():
        nonlocal last
        xg[0, 0] = hold(xg[0, 0], last)
        last = [xg[0, 0]]
        spread_from(2, cols)

    def activate_block(b):
        nonlocal last, kept
        got = [
            [[came[ring][s][b + j] for j in range(line - 1)] for s in range(2)] for ring in range(2)
        ]
        kept = activate(partial[b], got, kept, count * rows, b * rows, last)
        last = [kept[0]]

    def share_block(r):
        nonlocal last
        d, k = order[r]
        out_type = jnp.float32 if d == 0 else jnp.bfloat16
        shares[r] = share_of(kept, r * block, block, (w_out, w_in), out_type, last)
        last = [shares[r][0]]

    def swap(stream, k, later):
        nonlocal last
        array = shares[order.index((1, k))][stream]
        if later:
            array = hold(array, last)
            last = [array]
        swapped[stream, k] = over_dp(array)

    def pair_sum(stream, k):
        nonlocal last
        pairs[stream, k] = add_pair(shares[2 * k - 1][stream], swapped[stream, k], last)
        last = [pairs[stream, k]]

    def send_pair(stream, k, later):
        nonlocal last
        array = pairs[stream, k]
        if later:
            array = hold(array, last)
            last = [array]
        collected[stream, k] = over_col(array, k)

    def come_after(stream, k):
        last.append(collected[stream, k])

    todo = {}

    def at(t, window, *what):
        todo.setdefault((t, window), []).append(what)

    at(0, 0, gather_own)
    if per > 1:
        at(0, 1, project_blocks, (0, 1), [(i, own, i * rows, rows) for i in range(1, per)])
    staged = cols == 4 and per == 2
    if staged:
        at(REST_AT[0], REST_AT[1], gather_rest)
        for r, when in enumerate(PROJECT_AT):
            at(*when, project_one, r + 1)
    else:
        for r in range(1, len(order)):
            at(r * per - 1, 0, project_one, r)
    for b in range(count - 1):
        at(b + line - 1, 1, activate_block, b)
    for r in range(final):
        d, k = order[r]
        t = (r + 1) * per + line - 2
        at(t, 1, share_block, r)
        if d == 1 and r < final - 1:
            at(t, 1, swap, 0, k, False)
            at(t + 1, 1, pair_sum, 0, k)
            at(t + 1, 1, swap, 1, k, True)
            at(t + 2, 1, pair_sum, 1, k)
            at(t + 2, 1, send_pair, 0, k, True)
            at(t + 3, 1, come_after, 0, k)
            at(t + 3, 1, send_pair, 1, k, True)
            at(t + 4, 1, come_after, 1, k)
        elif d == 1:
            for stream in range(2):
                at(t, 1, swap, stream, k, False)
                at(t + 1, 1, pair_sum, stream, k)
                at(t + 1, 1, send_pair, stream, k, False)

    def run(t, window):
        for what, *rest in todo.pop((t, window), []):
            what(*rest)

    for t in range(count + line - 2):
        for stream in range(2):
            if t == 0:
                project_blocks((stream,), [(0, own, 0, rows)], True)
            step(stream, t)
            run(t, stream)
    for t, window in sorted(todo):
        run(t, window)
    activate_block(count - 1)
    share_block(final)
    for stream in range(2):
        swap(stream, 0, False)
    grad_w_in, grad_w_out = gradients([xg[d_k] for d_k in order], kept, last)

    terms = [
        [shares[0][s], *(collected[s, k] for k in range(1, cols)), swapped[s, 0]] for s in range(2)
    ]
    output, grad_x = total_of(terms, [grad_w_in])
    return (output, grad_x, grad_w_in[:, None, :], grad_w_out[None])


def solution(mesh):
    placed = (P(("dp", "col"), "row"), P("row", "col"), P("col", "row"), P(("dp", "col"), "row"))
    return jax.shard_map(
        functools.partial(on_device, mesh.shape["row"], mesh.shape["col"]),
        mesh=mesh,
        in_specs=placed,
        out_specs=(
            P(("dp", "col"), "row"),
            P(("dp", "col"), "row"),
            P("row", "col", "dp"),
            P("col", "dp", "row"),
        ),
        check_vma=False,
    )
```

time: 560 us -> 473 us (0.84)
  matrix products: 40.4 us -> 0 us
  waiting for transfers between devices: 107 us -> 79.5 us
  other arithmetic: 18.9 us -> 0 us
  local copies, waits for them, and re-layouts: 18.7 us -> 0 us
  Pallas kernels: 290 us -> 302 us
  starting transfers between devices: 72.4 us -> 82.3 us
    dot_general x4 -> x0, matrix products: 40.4 us -> none  [add_group(): lax.dot_general(*sides, (((0,), (0,)), ((), ())), preferred_element_type=...]
    ppermute x9, waiting for transfers between devices: 26 us -> 2.22 us  [over_col(): return lax.ppermute(x, 'col', [(i, i ^ k) for i in range(cols)])]
    convert_element_type x8 -> x0, other arithmetic: 18.9 us -> none  [the longest x6 13.4 us: pair_sum(): both = both.astype(jnp.bfloat16)]
    pallas_call x50, Pallas kernels: 169 us -> 184 us  [the longest x34 91.7 us: chain_step(): pl.pallas_call(body, in_specs=[ANY] * (2 + len(arrays) + len(after)), out...]
    ppermute x36 -> x72, starting transfers between devices: 54 us -> 67.7 us  [step(): lax.ppermute(send[ring], ('dp', 'row'), ring_pairs(ring))]
    unnamed x17 -> x0, local copies, waits for them, and re-layouts: 12 us -> none
    pallas_call x9 -> x10, Pallas kernels: 58.6 us -> 55.9 us  [project(): pl.pallas_call(body, grid_spec=pltpu.PrefetchScalarGridSpec(num_scalar_pr...]
    ppermute x36 -> x72, waiting for transfers between devices: 78.8 us -> 77.2 us  [step(): lax.ppermute(send[ring], ('dp', 'row'), ring_pairs(ring))]
  transfers between devices with their start and end apart: 57 -> 93, of which waited for: 21 -> 31; matrix products, arithmetic and copies ran while one was open for 13% -> 0% of each run, Pallas kernels for 47% -> 63%
where the time goes in v2:
time: 473 us; the launch traced here: 466 us
  Pallas kernels  302 us (64%)
  starting transfers between devices  82.3 us (17%)
  waiting for transfers between devices  79.5 us (17%)
    pallas_call x34, Pallas kernels, chain_step(): pl.pallas_call(body, in_specs=[ANY] * (2 + len(arrays) + len(after)), out...  91.7 us
    ppermute x72, waiting for transfers between devices, step(): lax.ppermute(send[ring], ('dp', 'row'), ring_pairs(ring))  77.2 us
    ppermute x72, starting transfers between devices, step(): lax.ppermute(send[ring], ('dp', 'row'), ring_pairs(ring))  67.7 us
    pallas_call x16, Pallas kernels, activate(): pl.pallas_call(body, in_specs=[ANY] * (len(given) + len(kept) + len(after...  60.1 us
    pallas_call x10, Pallas kernels, project(): pl.pallas_call(body, grid_spec=pltpu.PrefetchScalarGridSpec(num_scalar_pr...  55.9 us
    pallas_call x8, Pallas kernels, share_of(): pl.pallas_call(body, in_specs=[ANY] * (4 + len(after)), out_specs=[ANY] *...  50.6 us
    pallas_call x1, Pallas kernels, gradients(): pl.pallas_call(body, in_specs=[ANY] * (len(given) + len(after)), out_spec...  24.5 us
    ppermute x9, starting transfers between devices, over_col(): return lax.ppermute(x, 'col', [(i, i ^ k) for i in range(cols)])  13.4 us
  transfers between devices with their start and end apart: 93, of which 31 were waited for; matrix products, arithmetic and copies ran while one was open for 0% of the time, Pallas kernels for 63%

profile of v2, /device:TPU:0, one launch (start us, length us, event | category | flops | bytes accessed | tf_op | source)
XLA Modules:
  0.0 465.8 jit_solution(1817694530710324655)
XLA Ops:
  11.0 4.1 project.11
  17.1 5.6 %project.12 = (f32[128,2048]{1,0:T(8,128)}, f32[128,2048]{1,0:T(8,128)}) custom-call(s32[1]{0:T(128)} %bitcast.replica_ref, bf16[1024,4096]{1,0:T(8,128)(2,1)} %refs_3_.17, bf16[256,1024]{1,0:T(8,128)(2,1)} %refs_1_.7, bf16[4096,1024]{1,0:T(8,128)(2,1)} %refs_2_.31, bf16[256,1024]{1,0:T(8,128)(2,1)} %refs_3_.9, bf16[128,2048]{1,0:T(8,128)(2,1)} %get-tuple-element.145.refs_4_), custom_call_target="tpu_custom_call" | custom-call | flops 1024 | bytes 1024 | tf_op jit(solution)/shard_map/project/pallas_call | solution.py:77
  41.9 6.0 %project.13 = (f32[256,2048]{1,0:T(8,128)}, f32[256,2048]{1,0:T(8,128)}) custom-call(s32[1]{0:T(128)} %bitcast.replica_ref, bf16[1024,4096]{1,0:T(8,128)(2,1)} %refs_3_.17, bf16[2,256,1024]{2,1,0:T(8,128)(2,1)} %collective-permute-done.4.refs_1_.refs_3_, bf16[4096,1024]{1,0:T(8,128)(2,1)} %refs_2_.31, ...), custom_call_target="tpu_custom_call" | custom-call | flops 1024 | bytes 1024 | tf_op jit(solution)/shard_map/project/pallas_call | solution.py:77
  54.9 10.5 %collective-permute-done.11.refs_1_.refs_12_.refs_11_ = bf16[128,2048]{1,0:T(8,128)(2,1)} collective-permute-done((bf16[128,2048]{1,0:T(8,128)(2,1)}, bf16[128,2048]{1,0:T(8,128)(2,1)}, u32[]{:S(2)}, u32[]{:S(2)}) %collective-permute-start.11) | collective-permute-done | bytes 524320 | tf_op jit(solution)/shard_map/ppermute | solution.py:562
  68.7 6.1 %project.14 = (f32[256,2048]{1,0:T(8,128)}, f32[256,2048]{1,0:T(8,128)}) custom-call(s32[1]{0:T(128)} %bitcast.replica_ref, bf16[1024,4096]{1,0:T(8,128)(2,1)} %refs_3_.17, bf16[2,256,1024]{2,1,0:T(8,128)(2,1)} %collective-permute-done.9.refs_1_.refs_3_.refs_2_, bf16[4096,1024]{1,0:T(8,128)(2,1)} %refs_2_.31, ...), custom_call_target="tpu_custom_call" | custom-call | flops 1024 | bytes 1024 | tf_op jit(solution)/shard_map/project/pallas_call | solution.py:77
  85.4 5.4 %collective-permute-start.15 = (bf16[128,2048]{1,0:T(8,128)(2,1)}, bf16[128,2048]{1,0:T(8,128)(2,1)}, u32[]{:S(2)}, u32[]{:S(2)}) collective-permute-start(bf16[128,2048]{1,0:T(8,128)(2,1)} %get-tuple-element.162.refs_14_), channel_id=1, source_target_pairs={{0,4},{4,8},{8,12},{20,16},{24,20},{28,24},{12,28},{16,0},{1,5},{5... | collective-permute-start | bytes 1572872 | tf_op jit(solution)/shard_map/ppermute | solution.py:562
  100.6 6.1 %project.15 = (f32[256,2048]{1,0:T(8,128)}, f32[256,2048]{1,0:T(8,128)}) custom-call(s32[1]{0:T(128)} %bitcast.replica_ref, bf16[1024,4096]{1,0:T(8,128)(2,1)} %refs_3_.17, bf16[2,256,1024]{2,1,0:T(8,128)(2,1)} %collective-permute-done.18.refs_1_.refs_3_, bf16[4096,1024]{1,0:T(8,128)(2,1)} %refs_2_.31, ...), custom_call_target="tpu_custom_call" | custom-call | flops 1024 | bytes 1024 | tf_op jit(solution)/shard_map/project/pallas_call | solution.py:77
  115.2 6.4 %share_of.8 = (f32[256,1024]{1,0:T(8,128)}, f32[256,1024]{1,0:T(8,128)}) custom-call(bf16[2048,2048]{1,0:T(8,128)(2,1)} %get-tuple-element.171.refs_0_.refs_4_.refs_14_, bf16[2048,2048]{1,0:T(8,128)(2,1)} %get-tuple-element.172.refs_1_.refs_15_, bf16[4096,1024]{1,0:T(8,128)(2,1)} %refs_2_.31, bf16[1024,4096]{1,0:T(8,128)(2,1)} %refs_3_.17, ...), custom_call_target="tpu_custom_call" | custom-call | flops 1024 | bytes 1024 | tf_op jit(solution)/shard_map/share_of/pallas_call | solution.py:386
  127.5 6.1 %project.16 = (f32[256,2048]{1,0:T(8,128)}, f32[256,2048]{1,0:T(8,128)}) custom-call(s32[1]{0:T(128)} %bitcast.replica_ref, bf16[1024,4096]{1,0:T(8,128)(2,1)} %refs_3_.17, bf16[2,256,1024]{2,1,0:T(8,128)(2,1)} %collective-permute-done.24.refs_1_.refs_3_.refs_4_, bf16[4096,1024]{1,0:T(8,128)(2,1)} %refs_2_.31, ...), custom_call_target="tpu_custom_call" | custom-call | flops 1024 | bytes 1024 | tf_op jit(solution)/shard_map/project/pallas_call | solution.py:77
  161.1 6.5 %share_of.9 = (f32[256,1024]{1,0:T(8,128)}, f32[256,1024]{1,0:T(8,128)}) custom-call(bf16[2048,2048]{1,0:T(8,128)(2,1)} %get-tuple-element.186.refs_0_.refs_4_.refs_14_, bf16[2048,2048]{1,0:T(8,128)(2,1)} %get-tuple-element.187.refs_1_.refs_15_, bf16[4096,1024]{1,0:T(8,128)(2,1)} %refs_2_.31, bf16[1024,4096]{1,0:T(8,128)(2,1)} %refs_3_.17, ...), custom_call_target="tpu_custom_call" | custom-call | flops 1024 | bytes 1024 | tf_op jit(solution)/shard_map/share_of/pallas_call | solution.py:386
  172.6 6.1 %project.17 = (f32[256,2048]{1,0:T(8,128)}, f32[256,2048]{1,0:T(8,128)}) custom-call(s32[1]{0:T(128)} %bitcast.replica_ref, bf16[1024,4096]{1,0:T(8,128)(2,1)} %refs_3_.17, bf16[2,256,1024]{2,1,0:T(8,128)(2,1)} %collective-permute-done.33.refs_1_.refs_3_.refs_5_, bf16[4096,1024]{1,0:T(8,128)(2,1)} %refs_2_.31, ...), custom_call_target="tpu_custom_call" | custom-call | flops 1024 | bytes 1024 | tf_op jit(solution)/shard_map/project/pallas_call | solution.py:77
  205.7 6.2 %share_of.10 = (bf16[256,1024]{1,0:T(8,128)(2,1)}, bf16[256,1024]{1,0:T(8,128)(2,1)}) custom-call(bf16[2048,2048]{1,0:T(8,128)(2,1)} %get-tuple-element.201.refs_0_.refs_4_.refs_14_, bf16[2048,2048]{1,0:T(8,128)(2,1)} %get-tuple-element.202.refs_1_.refs_15_, bf16[4096,1024]{1,0:T(8,128)(2,1)} %refs_2_.31, bf16[1024,4096]{1,0:T(8,128)(2,1)} %refs_3_.17, ...), custom_call_target="tpu_custom_call" | custom-call | flops 1024 | bytes 1024 | tf_op jit(solution)/shard_map/share_of/pallas_call | solution.py:386
  217.0 6.1 %project.18 = (f32[256,2048]{1,0:T(8,128)}, f32[256,2048]{1,0:T(8,128)}) custom-call(s32[1]{0:T(128)} %bitcast.replica_ref, bf16[1024,4096]{1,0:T(8,128)(2,1)} %refs_3_.17, bf16[2,256,1024]{2,1,0:T(8,128)(2,1)} %collective-permute-done.42.refs_1_.refs_3_.refs_6_, bf16[4096,1024]{1,0:T(8,128)(2,1)} %refs_2_.31, ...), custom_call_target="tpu_custom_call" | custom-call | flops 1024 | bytes 1024 | tf_op jit(solution)/shard_map/project/pallas_call | solution.py:77
  253.4 6.4 %share_of.11 = (f32[256,1024]{1,0:T(8,128)}, f32[256,1024]{1,0:T(8,128)}) custom-call(bf16[2048,2048]{1,0:T(8,128)(2,1)} %get-tuple-element.218.rest_0_.refs_0_.refs_14_, bf16[2048,2048]{1,0:T(8,128)(2,1)} %get-tuple-element.219.refs_1_.refs_15_, bf16[4096,1024]{1,0:T(8,128)(2,1)} %refs_2_.31, bf16[1024,4096]{1,0:T(8,128)(2,1)} %refs_3_.17, ...), custom_call_target="tpu_custom_call" | custom-call | flops 1024 | bytes 1024 | tf_op jit(solution)/shard_map/share_of/pallas_call | solution.py:386
  264.8 6.1 %project.19 = (f32[256,2048]{1,0:T(8,128)}, f32[256,2048]{1,0:T(8,128)}) custom-call(s32[1]{0:T(128)} %bitcast.replica_ref, bf16[1024,4096]{1,0:T(8,128)(2,1)} %refs_3_.17, bf16[2,256,1024]{2,1,0:T(8,128)(2,1)} %collective-permute-done.54.refs_1_.refs_3_.refs_7_, bf16[4096,1024]{1,0:T(8,128)(2,1)} %refs_2_.31, ...), custom_call_target="tpu_custom_call" | custom-call | flops 1024 | bytes 1024 | tf_op jit(solution)/shard_map/project/pallas_call | solution.py:77
  298.5 6.2 %share_of.12 = (bf16[256,1024]{1,0:T(8,128)(2,1)}, bf16[256,1024]{1,0:T(8,128)(2,1)}) custom-call(bf16[2048,2048]{1,0:T(8,128)(2,1)} %get-tuple-element.233.refs_0_.refs_4_.refs_14_, bf16[2048,2048]{1,0:T(8,128)(2,1)} %get-tuple-element.234.refs_1_.refs_15_, bf16[4096,1024]{1,0:T(8,128)(2,1)} %refs_2_.31, bf16[1024,4096]{1,0:T(8,128)(2,1)} %refs_3_.17, ...), custom_call_target="tpu_custom_call" | custom-call | flops 1024 | bytes 1024 | tf_op jit(solution)/shard_map/share_of/pallas_call | solution.py:386
  328.2 5.4 %collective-permute-done.66.refs_0_.refs_7_.refs_6_.refs_5_ = bf16[128,2048]{1,0:T(8,128)(2,1)} collective-permute-done((bf16[128,2048]{1,0:T(8,128)(2,1)}, bf16[128,2048]{1,0:T(8,128)(2,1)}, u32[]{:S(2)}, u32[]{:S(2)}) %collective-permute-start.66) | collective-permute-done | bytes 524320 | tf_op jit(solution)/shard_map/ppermute | solution.py:562
  346.0 6.4 %share_of.13 = (f32[256,1024]{1,0:T(8,128)}, f32[256,1024]{1,0:T(8,128)}) custom-call(bf16[2048,2048]{1,0:T(8,128)(2,1)} %get-tuple-element.249.rest_0_.refs_0_.refs_14_, bf16[2048,2048]{1,0:T(8,128)(2,1)} %get-tuple-element.250.refs_1_.refs_15_, bf16[4096,1024]{1,0:T(8,128)(2,1)} %refs_2_.31, bf16[1024,4096]{1,0:T(8,128)(2,1)} %refs_3_.17, ...), custom_call_target="tpu_custom_call" | custom-call | flops 1024 | bytes 1024 | tf_op jit(solution)/shard_map/share_of/pallas_call | solution.py:386
  375.2 5.5 %collective-permute-done.75.refs_0_.refs_7_.refs_6_.refs_5_ = bf16[128,2048]{1,0:T(8,128)(2,1)} collective-permute-done((bf16[128,2048]{1,0:T(8,128)(2,1)}, bf16[128,2048]{1,0:T(8,128)(2,1)}, u32[]{:S(2)}, u32[]{:S(2)}) %collective-permute-start.75) | collective-permute-done | bytes 524320 | tf_op jit(solution)/shard_map/ppermute | solution.py:562
  390.2 6.2 %share_of.14 = (bf16[256,1024]{1,0:T(8,128)(2,1)}, bf16[256,1024]{1,0:T(8,128)(2,1)}) custom-call(bf16[2048,2048]{1,0:T(8,128)(2,1)} %get-tuple-element.262.refs_0_.refs_4_.refs_14_, bf16[2048,2048]{1,0:T(8,128)(2,1)} %get-tuple-element.263.refs_1_.refs_15_, bf16[4096,1024]{1,0:T(8,128)(2,1)} %refs_2_.31, bf16[1024,4096]{1,0:T(8,128)(2,1)} %refs_3_.17, ...), custom_call_target="tpu_custom_call" | custom-call | flops 1024 | bytes 1024 | tf_op jit(solution)/shard_map/share_of/pallas_call | solution.py:386
  417.0 5.7 %collective-permute-done.86.refs_7_ = bf16[128,2048]{1,0:T(8,128)(2,1)} collective-permute-done((bf16[128,2048]{1,0:T(8,128)(2,1)}, bf16[128,2048]{1,0:T(8,128)(2,1)}, u32[]{:S(2)}, u32[]{:S(2)}) %collective-permute-start.86) | collective-permute-done | bytes 524320 | tf_op jit(solution)/shard_map/ppermute | solution.py:562
  429.5 6.2 %share_of.15 = (bf16[256,1024]{1,0:T(8,128)(2,1)}, bf16[256,1024]{1,0:T(8,128)(2,1)}) custom-call(bf16[2048,2048]{1,0:T(8,128)(2,1)} %get-tuple-element.275.refs_0_.refs_4_.refs_8_, bf16[2048,2048]{1,0:T(8,128)(2,1)} %get-tuple-element.276.refs_1_.refs_9_, bf16[4096,1024]{1,0:T(8,128)(2,1)} %refs_2_.31, bf16[1024,4096]{1,0:T(8,128)(2,1)} %refs_3_.17, ...), custom_call_target="tpu_custom_call" | custom-call | flops 1024 | bytes 1024 | tf_op jit(solution)/shard_map/share_of/pallas_call | solution.py:386
  436.3 24.5 %gradients.1 = (bf16[1024,2048]{1,0:T(8,128)(2,1)}, bf16[2048,1024]{1,0:T(8,128)(2,1)}) custom-call(bf16[2,256,1024]{2,1,0:T(8,128)(2,1)} %hold.7.refs_5_.refs_0_, bf16[2,256,1024]{2,1,0:T(8,128)(2,1)} %collective-permute-done.4.refs_1_.refs_3_, bf16[2,256,1024]{2,1,0:T(8,128)(2,1)} %collective-permute-done.9.refs_1_.refs_3_.refs_2_, ...), custom_call_target="tpu_custom_call" | custom-call | flops 1024 | bytes 1024 | tf_op jit(solution)/shard_map/gradients/pallas_call | solution.py:478
  460.9 4.5 total_of.1
  (246 shorter events, 299.5 us)
Async XLA Ops:
  6.4 26.5 %collective-permute-start.4 = (bf16[2,256,1024]{2,1,0:T(8,128)(2,1)}, bf16[2,256,1024]{2,1,0:T(8,128)(2,1)}, u32[]{:S(2)}, u32[]{:S(2)}) collective-permute-start(bf16[2,256,1024]{2,1,0:T(8,128)(2,1)} %pack.1.refs_2_.refs_0_), channel_id=1, source_target_pairs={{0,1},{1,0},{2,3},{3,2},{4,5},{5,4},{6,7},{7,6},{8,9},{9,8},{10,11... | collective-permute-start | bytes 3145736 | tf_op jit(solution)/shard_map/ppermute | solution.py:518
  32.9 35.5 %collective-permute-start.9 = (bf16[2,256,1024]{2,1,0:T(8,128)(2,1)}, bf16[2,256,1024]{2,1,0:T(8,128)(2,1)}, u32[]{:S(2)}, u32[]{:S(2)}) collective-permute-start(bf16[2,256,1024]{2,1,0:T(8,128)(2,1)} %collective-permute-done.4.refs_1_.refs_3_), channel_id=1, source_target_pairs={{0,16},{16,0},{1,17},{17,1},{2,18},{18,2},{3,19},{19,3},{4,20},{20... | collective-permute-start | bytes 3145736 | tf_op jit(solution)/shard_map/ppermute | solution.py:515
  51.3 31.3 %collective-permute-start.18 = (bf16[2,256,1024]{2,1,0:T(8,128)(2,1)}, bf16[2,256,1024]{2,1,0:T(8,128)(2,1)}, u32[]{:S(2)}, u32[]{:S(2)}) collective-permute-start(bf16[2,256,1024]{2,1,0:T(8,128)(2,1)} %hold.7.refs_5_.refs_0_), channel_id=1, source_target_pairs={{0,2},{1,3},{2,0},{3,1},{4,6},{5,7},{6,4},{7,5},{8,10},{9,11},{10,... | collective-permute-start | bytes 3145736 | tf_op jit(solution)/shard_map/ppermute | solution.py:518
  82.6 44.3 %collective-permute-start.24 = (bf16[2,256,1024]{2,1,0:T(8,128)(2,1)}, bf16[2,256,1024]{2,1,0:T(8,128)(2,1)}, u32[]{:S(2)}, u32[]{:S(2)}) collective-permute-start(bf16[2,256,1024]{2,1,0:T(8,128)(2,1)} %collective-permute-done.18.refs_1_.refs_3_), channel_id=1, source_target_pairs={{0,16},{16,0},{1,17},{17,1},{2,18},{18,2},{3,19},{19,3},{4,20},{20... | collective-permute-start | bytes 3145736 | tf_op jit(solution)/shard_map/ppermute | solution.py:515
  99.4 22.2 %collective-permute-start.19 = (bf16[128,2048]{1,0:T(8,128)(2,1)}, bf16[128,2048]{1,0:T(8,128)(2,1)}, u32[]{:S(2)}, u32[]{:S(2)}) collective-permute-start(bf16[128,2048]{1,0:T(8,128)(2,1)} %get-tuple-element.168.refs_4_), channel_id=1, source_target_pairs={{0,4},{4,8},{8,12},{20,16},{24,20},{28,24},{12,28},{16,0},{1,5},{5... | collective-permute-start | bytes 1572872 | tf_op jit(solution)/shard_map/ppermute | solution.py:562
  110.6 22.9 %collective-permute-start.22 = (bf16[128,2048]{1,0:T(8,128)(2,1)}, bf16[128,2048]{1,0:T(8,128)(2,1)}, u32[]{:S(2)}, u32[]{:S(2)}) collective-permute-start(bf16[128,2048]{1,0:T(8,128)(2,1)} %get-tuple-element.170.refs_16_), channel_id=1, source_target_pairs={{0,4},{4,8},{8,12},{20,16},{24,20},{28,24},{12,28},{16,0},{1,5},{5... | collective-permute-start | bytes 1572872 | tf_op jit(solution)/shard_map/ppermute | solution.py:562
  126.9 45.6 %collective-permute-start.33 = (bf16[2,256,1024]{2,1,0:T(8,128)(2,1)}, bf16[2,256,1024]{2,1,0:T(8,128)(2,1)}, u32[]{:S(2)}, u32[]{:S(2)}) collective-permute-start(bf16[2,256,1024]{2,1,0:T(8,128)(2,1)} %collective-permute-done.18.refs_1_.refs_3_), channel_id=1, source_target_pairs={{0,1},{1,0},{2,3},{3,2},{4,5},{5,4},{6,7},{7,6},{8,9},{9,8},{10,11... | collective-permute-start | bytes 3145736 | tf_op jit(solution)/shard_map/ppermute | solution.py:518
  144.8 22.8 %collective-permute-start.28 = (bf16[128,2048]{1,0:T(8,128)(2,1)}, bf16[128,2048]{1,0:T(8,128)(2,1)}, u32[]{:S(2)}, u32[]{:S(2)}) collective-permute-start(bf16[128,2048]{1,0:T(8,128)(2,1)} %get-tuple-element.184.refs_5_), channel_id=1, source_target_pairs={{0,4},{4,8},{8,12},{20,16},{24,20},{28,24},{12,28},{16,0},{1,5},{5... | collective-permute-start | bytes 1572872 | tf_op jit(solution)/shard_map/ppermute | solution.py:562
  155.2 23.4 %collective-permute-start.31 = (bf16[128,2048]{1,0:T(8,128)(2,1)}, bf16[128,2048]{1,0:T(8,128)(2,1)}, u32[]{:S(2)}, u32[]{:S(2)}) collective-permute-start(bf16[128,2048]{1,0:T(8,128)(2,1)} %get-tuple-element.185.refs_16_), channel_id=1, source_target_pairs={{0,4},{4,8},{8,12},{20,16},{24,20},{28,24},{12,28},{16,0},{1,5},{5... | collective-permute-start | bytes 1572872 | tf_op jit(solution)/shard_map/ppermute | solution.py:562
  172.5 44.4 %collective-permute-start.42 = (bf16[2,256,1024]{2,1,0:T(8,128)(2,1)}, bf16[2,256,1024]{2,1,0:T(8,128)(2,1)}, u32[]{:S(2)}, u32[]{:S(2)}) collective-permute-start(bf16[2,256,1024]{2,1,0:T(8,128)(2,1)} %collective-permute-done.33.refs_1_.refs_3_.refs_5_), channel_id=1, source_target_pairs={{0,16},{16,0},{1,17},{17,1},{2,18},{18,2},{3,19},{19,3},{4,20},{20... | collective-permute-start | bytes 3145736 | tf_op jit(solution)/shard_map/ppermute | solution.py:515
  227.8 37.0 %collective-permute-start.54 = (bf16[2,256,1024]{2,1,0:T(8,128)(2,1)}, bf16[2,256,1024]{2,1,0:T(8,128)(2,1)}, u32[]{:S(2)}, u32[]{:S(2)}) collective-permute-start(bf16[2,256,1024]{2,1,0:T(8,128)(2,1)} %hold.7.refs_5_.refs_0_), channel_id=1, source_target_pairs={{0,16},{16,0},{1,17},{17,1},{2,18},{18,2},{3,19},{19,3},{4,20},{20... | collective-permute-start | bytes 3145736 | tf_op jit(solution)/shard_map/ppermute | solution.py:515
  244.8 26.1 %collective-permute-start.52 = (bf16[128,2048]{1,0:T(8,128)(2,1)}, bf16[128,2048]{1,0:T(8,128)(2,1)}, u32[]{:S(2)}, u32[]{:S(2)}) collective-permute-start(bf16[128,2048]{1,0:T(8,128)(2,1)} %get-tuple-element.217.refs_16_), channel_id=1, source_target_pairs={{0,4},{4,8},{8,12},{20,16},{24,20},{28,24},{12,28},{16,0},{1,5},{5... | collective-permute-start | bytes 1572872 | tf_op jit(solution)/shard_map/ppermute | solution.py:562
  246.6 24.3 %collective-permute-start.53 = (bf16[128,2048]{1,0:T(8,128)(2,1)}, bf16[128,2048]{1,0:T(8,128)(2,1)}, u32[]{:S(2)}, u32[]{:S(2)}) collective-permute-start(bf16[128,2048]{1,0:T(8,128)(2,1)} %get-tuple-element.223), channel_id=1, source_target_pairs={{16,20},{20,24},{24,28},{4,0},{8,4},{12,8},{28,12},{0,16},{17,21},... | collective-permute-start | bytes 1572872 | tf_op jit(solution)/shard_map/ppermute | solution.py:562
  252.5 27.0 %collective-permute-start.48 = (bf16[256,1024]{1,0:T(8,128)(2,1)}, bf16[256,1024]{1,0:T(8,128)(2,1)}, u32[]{:S(2)}, u32[]{:S(2)}) collective-permute-start(bf16[256,1024]{1,0:T(8,128)(2,1)} %hold.9.refs_4_), channel_id=1, source_target_pairs={{0,1},{1,0},{2,3},{3,2},{4,5},{5,4},{6,7},{7,6},{8,9},{9,8},{10,11... | collective-permute-start | bytes 1572872 | tf_op jit(solution)/shard_map/ppermute | solution.py:518
  320.4 22.7 %collective-permute-start.64 = (bf16[256,1024]{1,0:T(8,128)(2,1)}, bf16[256,1024]{1,0:T(8,128)(2,1)}, u32[]{:S(2)}, u32[]{:S(2)}) collective-permute-start(bf16[256,1024]{1,0:T(8,128)(2,1)} %hold.11.refs_5_), channel_id=1, source_target_pairs={{0,16},{16,0},{1,17},{17,1},{2,18},{18,2},{3,19},{19,3},{4,20},{20... | collective-permute-start | bytes 1572872 | tf_op jit(solution)/shard_map/ppermute | solution.py:515
  327.6 24.7 %collective-permute-start.70 = (bf16[128,2048]{1,0:T(8,128)(2,1)}, bf16[128,2048]{1,0:T(8,128)(2,1)}, u32[]{:S(2)}, u32[]{:S(2)}) collective-permute-start(bf16[128,2048]{1,0:T(8,128)(2,1)} %get-tuple-element.247.refs_5_), channel_id=1, source_target_pairs={{0,4},{4,8},{8,12},{20,16},{24,20},{28,24},{12,28},{16,0},{1,5},{5... | collective-permute-start | bytes 1572872 | tf_op jit(solution)/shard_map/ppermute | solution.py:562
  327.7 24.7 %collective-permute-start.71 = (bf16[128,2048]{1,0:T(8,128)(2,1)}, bf16[128,2048]{1,0:T(8,128)(2,1)}, u32[]{:S(2)}, u32[]{:S(2)}) collective-permute-start(bf16[128,2048]{1,0:T(8,128)(2,1)} %get-tuple-element.252), channel_id=1, source_target_pairs={{16,20},{20,24},{24,28},{4,0},{8,4},{12,8},{28,12},{0,16},{17,21},... | collective-permute-start | bytes 1572872 | tf_op jit(solution)/shard_map/ppermute | solution.py:562
  365.4 24.9 %collective-permute-start.78 = (bf16[256,1024]{1,0:T(8,128)(2,1)}, bf16[256,1024]{1,0:T(8,128)(2,1)}, u32[]{:S(2)}, u32[]{:S(2)}) collective-permute-start(bf16[256,1024]{1,0:T(8,128)(2,1)} %hold.13.refs_4_), channel_id=1, source_target_pairs={{0,2},{1,3},{2,0},{3,1},{4,6},{5,7},{6,4},{7,5},{8,10},{9,11},{10,... | collective-permute-start | bytes 1572872 | tf_op jit(solution)/shard_map/ppermute | solution.py:518
  374.8 22.3 %collective-permute-start.82 = (bf16[128,2048]{1,0:T(8,128)(2,1)}, bf16[128,2048]{1,0:T(8,128)(2,1)}, u32[]{:S(2)}, u32[]{:S(2)}) collective-permute-start(bf16[128,2048]{1,0:T(8,128)(2,1)} %get-tuple-element.265), channel_id=1, source_target_pairs={{16,20},{20,24},{24,28},{4,0},{8,4},{12,8},{28,12},{0,16},{17,21},... | collective-permute-start | bytes 1572872 | tf_op jit(solution)/shard_map/ppermute | solution.py:562
  399.8 25.2 %collective-permute-start.85 = (bf16[128,2048]{1,0:T(8,128)(2,1)}, bf16[128,2048]{1,0:T(8,128)(2,1)}, u32[]{:S(2)}, u32[]{:S(2)}) collective-permute-start(bf16[128,2048]{1,0:T(8,128)(2,1)} %get-tuple-element.267.refs_3_), channel_id=1, source_target_pairs={{0,4},{4,8},{8,12},{20,16},{24,20},{28,24},{12,28},{16,0},{1,5},{5... | collective-permute-start | bytes 1572872 | tf_op jit(solution)/shard_map/ppermute | solution.py:562
  413.2 47.6 %collective-permute-start.84 = (bf16[256,1024]{1,0:T(8,128)(2,1)}, bf16[256,1024]{1,0:T(8,128)(2,1)}, u32[]{:S(2)}, u32[]{:S(2)}) collective-permute-start(bf16[256,1024]{1,0:T(8,128)(2,1)} %add_pair.10.rest_0_), channel_id=1, source_target_pairs={{0,3},{1,2},{2,1},{3,0},{4,7},{5,6},{6,5},{7,4},{8,11},{9,10},{10,... | collective-permute-start | bytes 1572872 | tf_op jit(solution)/shard_map/ppermute | solution.py:518
  422.7 38.1 %collective-permute-start.91 = (bf16[256,1024]{1,0:T(8,128)(2,1)}, bf16[256,1024]{1,0:T(8,128)(2,1)}, u32[]{:S(2)}, u32[]{:S(2)}) collective-permute-start(bf16[256,1024]{1,0:T(8,128)(2,1)} %add_pair.11.refs_16_), channel_id=1, source_target_pairs={{0,3},{1,2},{2,1},{3,0},{4,7},{5,6},{6,5},{7,4},{8,11},{9,10},{10,... | collective-permute-start | bytes 1572872 | tf_op jit(solution)/shard_map/ppermute | solution.py:518
  435.7 25.1 %collective-permute-start.90 = (bf16[256,1024]{1,0:T(8,128)(2,1)}, bf16[256,1024]{1,0:T(8,128)(2,1)}, u32[]{:S(2)}, u32[]{:S(2)}) collective-permute-start(bf16[256,1024]{1,0:T(8,128)(2,1)} %get-tuple-element.277.refs_10_), channel_id=1, source_target_pairs={{0,16},{16,0},{1,17},{17,1},{2,18},{18,2},{3,19},{19,3},{4,20},{20... | collective-permute-start | bytes 1572872 | tf_op jit(solution)/shard_map/ppermute | solution.py:515
  435.9 25.0 %collective-permute-start.92 = (bf16[256,1024]{1,0:T(8,128)(2,1)}, bf16[256,1024]{1,0:T(8,128)(2,1)}, u32[]{:S(2)}, u32[]{:S(2)}) collective-permute-start(bf16[256,1024]{1,0:T(8,128)(2,1)} %get-tuple-element.279), channel_id=1, source_target_pairs={{0,16},{16,0},{1,17},{17,1},{2,18},{18,2},{3,19},{19,3},{4,20},{20... | collective-permute-start | bytes 1572872 | tf_op jit(solution)/shard_map/ppermute | solution.py:515
  (69 other events, 1201.6 us)
